TPU v7x, 256 devices: a whole 4x4x8 slice. The times are simulated.
256 devices in a mesh: rep: 16 (over z_hi, y), fsdp: 16 (over z_lo, x, core).
Axes of the slice: x: 4, y: 4, z: 8 (z_hi: 4, z_lo: 2; z = z_hi * 2 + z_lo), core: 2. Of those that a mesh axis runs over, the one named last changes fastest.
Arguments:
- query_states: bfloat16 [65536, 2048], P(('rep', 'fsdp')), may hold values from -6 to 6
- key_states: bfloat16 [65536, 1024], P(('rep', 'fsdp')), may hold values from -6 to 6
- value_states: bfloat16 [65536, 1024], P(('rep', 'fsdp')), may hold values from -6 to 6
- output_grad: bfloat16 [65536, 2304], P(('rep', 'fsdp')), may hold values from -6 to 6
- out_weight: bfloat16 [16, 2048, 2304], P('rep', 'fsdp'), may hold values from -0.125 to 0.125
- pseudo_grad: float32 [16, 2048, 2304], P('rep', 'fsdp'), may hold values from -6 to 6
- anchor: float32 [2048, 2304], P('fsdp'), may hold values from -6 to 6
- momentum: float32 [2048, 2304], P('fsdp', 'rep'), may hold values from -6 to 6
- local_weight: bfloat16 [16, 2048, 2304], P('rep', 'fsdp'), may hold values from -6 to 6
Outputs:
- branch_out: bfloat16 [65536, 2304], P(('rep', 'fsdp'))
- grad_q: bfloat16 [65536, 2048], P(('rep', 'fsdp'))
- grad_k: bfloat16 [65536, 1024], P(('rep', 'fsdp'))
- grad_v: bfloat16 [65536, 1024], P(('rep', 'fsdp'))
- weight_grad: bfloat16 [16, 2048, 2304], P('rep', 'fsdp')
- anchor_new: float32 [2048, 2304], P('fsdp')
- momentum_new: float32 [2048, 2304], P('fsdp', 'rep')
- merged: bfloat16 [16, 2048, 2304], P('rep', 'fsdp')
All inputs are finite; a program needn't handle non-finite values.
Results may differ from a plain program's by a relative error of at most 0.022.
Values may be sent and summed in bfloat16 or wider, within the bound.
No kernel may reach another device: no remote copies, remote signals or barrier semaphores. Data moves between devices by JAX's collectives and lax.ppermute only.
A program may use at most 128 MiB of HBM per device.

v0:
```python
import jax
import jax.numpy as jnp
from jax import lax
from jax.sharding import PartitionSpec as P

HEADS = 16
KV_HEADS = 8
HEAD_DIM = 128


query_scale = 1.0 / 12.0
outer_rate = 0.7
outer_moment = 0.9
mix_factor = 0.5


def causal_softmax(query_heads, key_heads):
    length = query_heads.shape[0]
    scores = (
        jnp.einsum("igrd,jgd->grij", query_heads, key_heads, preferred_element_type=jnp.float32)
        * query_scale
    )
    allowed = jnp.arange(length)[:, None] >= jnp.arange(length)[None, :]
    scores = jnp.where(allowed, scores, -jnp.inf)
    highest = jnp.max(scores, axis=-1, keepdims=True)
    exponent_terms = jnp.exp(scores - highest)
    return exponent_terms / jnp.sum(exponent_terms, axis=-1, keepdims=True)


def on_device(
    query_states,
    key_states,
    value_states,
    output_grad,
    out_weight,
    pseudo_grad,
    anchor,
    momentum,
    local_weight,
):
    length = query_states.shape[0]
    per_group = HEADS // KV_HEADS
    query_heads = query_states.reshape(length, KV_HEADS, per_group, HEAD_DIM)
    key_heads = key_states.reshape(length, KV_HEADS, HEAD_DIM)
    value_heads = value_states.reshape(length, KV_HEADS, HEAD_DIM)
    attention = causal_softmax(query_heads, key_heads)
    attention_b = attention.astype(jnp.bfloat16)
    mixed_rows = jnp.einsum(
        "grij,jgd->igrd", attention_b, value_heads, preferred_element_type=jnp.float32
    )
    mixed_rows = mixed_rows.reshape(length, HEADS * HEAD_DIM).astype(jnp.bfloat16)
    own_rows = out_weight[0]
    full_weight = lax.all_gather(own_rows, "fsdp", axis=0, tiled=True)
    branch = jnp.dot(mixed_rows, full_weight, preferred_element_type=jnp.float32)
    grad_mixed = lax.dot_general(
        output_grad, full_weight, (((1,), (1,)), ((), ())), preferred_element_type=jnp.float32
    )
    branch_out = branch.astype(jnp.bfloat16)
    grad_mixed = grad_mixed.astype(jnp.bfloat16)
    weight_grad = lax.psum_scatter(
        lax.dot_general(
            mixed_rows, output_grad, (((0,), (0,)), ((), ())), preferred_element_type=jnp.float32
        ).astype(jnp.bfloat16),
        "fsdp",
        scatter_dimension=0,
        tiled=True,
    ).astype(jnp.float32)
    weight_grad = weight_grad.astype(jnp.bfloat16)[None]
    grad_heads = grad_mixed.reshape(length, KV_HEADS, per_group, HEAD_DIM)
    grad_probs = jnp.einsum(
        "igrd,jgd->grij", grad_heads, value_heads, preferred_element_type=jnp.float32
    )
    row_term = jnp.sum(attention * grad_probs, axis=-1, keepdims=True)
    grad_scores = (attention * (grad_probs - row_term) * query_scale).astype(jnp.bfloat16)
    grad_query = jnp.einsum(
        "grij,jgd->igrd", grad_scores, key_heads, preferred_element_type=jnp.float32
    )
    grad_key = jnp.einsum(
        "grij,igrd->jgd", grad_scores, query_heads, preferred_element_type=jnp.float32
    )
    grad_value = jnp.einsum(
        "grij,igrd->jgd", attention_b, grad_heads, preferred_element_type=jnp.float32
    )
    grad_query = grad_query.reshape(length, HEADS * HEAD_DIM).astype(jnp.bfloat16)
    grad_key = grad_key.reshape(length, KV_HEADS * HEAD_DIM).astype(jnp.bfloat16)
    grad_value = grad_value.reshape(length, KV_HEADS * HEAD_DIM).astype(jnp.bfloat16)
    replicas = lax.axis_size("rep")
    position = lax.axis_index("rep")
    share_width = momentum.shape[1]
    own_delta = pseudo_grad[0]
    mean_delta = lax.psum(own_delta.astype(jnp.bfloat16), "rep").astype(jnp.float32) / replicas
    mean_share = lax.dynamic_slice_in_dim(mean_delta, position * share_width, share_width, 1)
    momentum_new = outer_moment * momentum + mean_share
    momentum_full = lax.all_gather(
        momentum_new.astype(jnp.bfloat16), "rep", axis=1, tiled=True
    ).astype(momentum_new.dtype)
    anchor_new = anchor - outer_rate * (outer_moment * momentum_full + mean_delta)
    merged = (mix_factor * local_weight[0].astype(jnp.float32) + mix_factor * anchor_new).astype(
        jnp.bfloat16
    )[None]
    return (
        branch_out,
        grad_query,
        grad_key,
        grad_value,
        weight_grad,
        anchor_new,
        momentum_new,
        merged,
    )


def solution(mesh):
    return jax.shard_map(
        on_device,
        mesh=mesh,
        in_specs=(
            P(("rep", "fsdp"), None),
            P(("rep", "fsdp"), None),
            P(("rep", "fsdp"), None),
            P(("rep", "fsdp"), None),
            P("rep", "fsdp", None),
            P("rep", "fsdp", None),
            P("fsdp", None),
            P("fsdp", "rep"),
            P("rep", "fsdp", None),
        ),
        out_specs=(
            P(("rep", "fsdp"), None),
            P(("rep", "fsdp"), None),
            P(("rep", "fsdp"), None),
            P(("rep", "fsdp"), None),
            P("rep", "fsdp", None),
            P("fsdp", None),
            P("fsdp", "rep"),
            P("rep", "fsdp", None),
        ),
        check_vma=False,
    )
```

profile of v0, /device:TPU:8, one launch (start us, length us, event | category | flops | bytes accessed | tf_op | source)
XLA Modules:
  0.0 310.5 jit_solution(10377038245676244704)
XLA Ops:
  8.1 2.4 copy.29
  11.2 1.1 copy.56
  12.8 1.7 copy.54
  14.5 3.5 %fusion.43 = (f32[8,2,256]{2,1,0:T(2,128)S(1)}, f32[8,2,256,256]{2,3,1,0:T(8,128)}) fusion(pred[256,256]{0,1:T(8,128)(4,1)S(1)} %iota_compare_fusion, bf16[256,8,128,1]{0,2,3,1:T(8,128)(2,1)S(1)} %copy.41, bf16[256,8,2,128]{0,3,2,1:T(8,128)(2,1)S(1)} %bitcast.115), kind=kOutput, calls=%fused_computation.52 | convolution fusion | flops 272630016 | bytes 5849088 | tf_op jit(solution)/shard_map/sub | solution.py:26
  18.0 2.8 convolution_convert_fusion.1
  20.8 5.1 %convolution_convert_fusion = bf16[2048,2304]{1,0:T(8,128)(2,1)} fusion(bf16[256,2048]{0,1:T(8,128)(2,1)S(1)} %bitcast.107, bf16[256,2304]{1,0:T(8,128)(2,1)S(1)} %copy-done), kind=kOutput, calls=%fused_computation.2 | convolution fusion | flops 2420637696 | bytes 11665408 | tf_op jit(solution)/shard_map/dot_general | solution.py:61
  25.9 1.7 copy.30
  27.6 172.1 %all-reduce.2.cloned.1.call-done = bf16[128,2304]{0,1:T(8,128)(2,1)} async-done(((bf16[128,2304]{0,1:T(8,128)(2,1)}), bf16[128,2304]{0,1:T(8,128)(2,1)}) %all-reduce.2.cloned.1.call-update) | async-done | bytes 589840 | tf_op jit(solution)/shard_map/psum | solution.py:91
  199.8 1.1 convert_multiply_fusion
  200.9 0.7 fusion.42
  201.6 48.4 %all_gather.7 = bf16[128,2304]{0,1:T(8,128)(2,1)S(1)} all-gather(bf16[128,144]{0,1:T(8,128)(2,1)S(1)} %get-tuple-element.16), channel_id=1, replica_groups=mesh['rep'=16,'fsdp'=16] {'rep'}, dimensions={1}, use_global_device_ids=true | all-gather | bytes 626688 | tf_op jit(solution)/shard_map/all_gather | solution.py:94
  249.9 2.4 multiply_subtract_fusion
  252.3 1.6 copy.35
  253.9 2.4 fusion.30
  256.4 7.3 %fusion.13 = bf16[256,2048]{1,0:T(8,128)(2,1)} fusion(bf16[256,2304]{1,0:T(8,128)(2,1)S(1)} %copy-done, bf16[1,2048,2304]{2,1,0:T(8,128)(2,1)} %all-gather.3.cloned.1.call-done), kind=kOutput, calls=%fused_computation.16 | convolution fusion | flops 2416443392 | bytes 11665408 | tf_op jit(solution)/shard_map/dot_general | solution.py:55
  263.7 2.3 copy.55
  265.9 4.1 %fusion.32 = f32[8,256,2,256]{1,3,2,0:T(8,128)} fusion(bf16[256,8,2,128]{0,3,2,1:T(8,128)(2,1)} %bitcast.109, bf16[256,8,128,1]{2,1,0,3:T(8,128)(2,1)} %bitcast.114), kind=kOutput, calls=%fused_computation.40 | convolution fusion | flops 268435456 | bytes 5767168 | tf_op jit(solution)/shard_map/igrd,jgd->grij/dot_general | solution.py:70
  270.0 7.7 %fusion.22 = bf16[8,2,256,128]{2,3,1,0:T(8,128)(2,1)S(1)} fusion(bf16[256,8,128,1]{0,2,3,1:T(8,128)(2,1)} %copy-done.6, f32[8,256,2,256]{1,3,2,0:T(8,128)} %fusion.32, f32[8,2,256,256]{2,3,1,0:T(8,128)} %get-tuple-element.19, f32[8,2,256]{2,1,0:T(2,128)S(1)} %get-tuple-element.18), kind=kOutput, calls=%fused_computation.25 | convolution fusion | flops 276304128 | bytes 9977856 | tf_op jit(solution)/shard_map/grij,jgd->igrd/dot_general | solution.py:75
  277.7 1.4 copy.32
  279.1 8.7 %fusion.25 = bf16[8,256,128]{1,2,0:T(8,128)(2,1)} fusion(bf16[256,8,2,128]{0,3,2,1:T(8,128)(2,1)} %bitcast.116, f32[8,256,2,256]{1,3,2,0:T(8,128)} %fusion.32, f32[8,2,256,256]{2,3,1,0:T(8,128)} %get-tuple-element.19, f32[8,2,256]{2,1,0:T(2,128)S(1)} %get-tuple-element.18), kind=kOutput, calls=%fused_computation.29 | convolution fusion | flops 276041984 | bytes 9977856 | tf_op jit(solution)/shard_map/grij,igrd->jgd/dot_general | solution.py:78
  287.8 2.0 copy.33
  289.8 3.8 %fusion.24 = bf16[8,128,256]{2,1,0:T(8,128)(2,1)} fusion(bf16[256,8,2,128]{0,3,2,1:T(8,128)(2,1)S(1)} %bitcast.110, f32[8,2,256,256]{2,3,1,0:T(8,128)} %get-tuple-element.19, f32[8,2,256]{2,1,0:T(2,128)S(1)} %get-tuple-element.18), kind=kOutput, calls=%fused_computation.28 | convolution fusion | flops 270794752 | bytes 5783552 | tf_op jit(solution)/shard_map/grij,igrd->jgd/dot_general | solution.py:81
  293.7 2.0 copy.34
  295.7 7.3 %fusion.9 = bf16[256,2304]{1,0:T(8,128)(2,1)} fusion(bf16[256,2048]{0,1:T(8,128)(2,1)S(1)} %bitcast.108, bf16[1,2048,2304]{2,1,0:T(8,128)(2,1)} %all-gather.3.cloned.1.call-done), kind=kOutput, calls=%fused_computation.14 | convolution fusion | flops 2416508928 | bytes 11665408 | tf_op jit(solution)/shard_map/dot_general | solution.py:54
  (27 shorter events, 1.2 us)
Async XLA Ops:
  8.0 12.8 %copy-start = (bf16[256,2304]{1,0:T(8,128)(2,1)S(1)}, bf16[256,2304]{1,0:T(8,128)(2,1)}, u32[]{:S(2)}) copy-start(bf16[256,2304]{1,0:T(8,128)(2,1)} %param.12) | copy-start | bytes 3538948
  8.0 4.3 %copy-start.5 = (bf16[256,1024]{1,0:T(8,128)(2,1)S(1)}, bf16[256,1024]{1,0:T(8,128)(2,1)}, u32[]{:S(2)}) copy-start(bf16[256,1024]{1,0:T(8,128)(2,1)} %param.10) | copy-start | bytes 1572868
  8.0 191.7 %all-reduce.2.cloned.1.call-start = ((), (), s32[]{:S(2)}) async-start(), calls=%async_computation.2 | async-start | bytes 1179648 | tf_op jit(solution)/shard_map/psum | solution.py:91
  10.5 245.8 %all-gather.3.cloned.1.call-start = ((), (), s32[]{:S(2)}) async-start(), calls=%async_computation.3 | async-start | bytes 10027008 | tf_op jit(solution)/shard_map/all_gather | solution.py:53
  11.1 291.9 %reduce-scatter.2.cloned.1.call-start = ((), (), s32[]{:S(2)}) async-start(), calls=%async_computation.1 | async-start | bytes 10027008 | tf_op jit(solution)/shard_map/reduce_scatter | solution.py:60
  12.3 5.7 %copy-start.3 = (bf16[32,8,8,128]{3,2,1,0:T(8,128)(2,1)}, bf16[32,8,8,128]{3,2,1,0:T(8,128)(2,1)S(1)}, u32[]{:S(2)}) copy-start(bf16[32,8,8,128]{3,2,1,0:T(8,128)(2,1)S(1)} %copy.56) | copy-start | bytes 1572868
  12.8 5.2 %copy-start.6 = (bf16[256,8,128,1]{0,2,3,1:T(8,128)(2,1)}, bf16[256,8,128,1]{0,2,3,1:T(8,128)(2,1)S(1)}, u32[]{:S(2)}) copy-start(bf16[256,8,128,1]{0,2,3,1:T(8,128)(2,1)S(1)} %copy.41) | copy-start | bytes 1572868
  14.5 3.6 %copy-start.4 = (bf16[256,2048]{0,1:T(8,128)(2,1)}, bf16[256,2048]{0,1:T(8,128)(2,1)S(1)}, u32[]{:S(2)}) copy-start(bf16[256,2048]{0,1:T(8,128)(2,1)S(1)} %copy.54) | copy-start | bytes 3145732
  25.9 175.0 %copy-start.7 = (f32[128,144]{0,1:T(8,128)S(1)}, f32[128,144]{0,1:T(8,128)}, u32[]{:S(2)}) copy-start(f32[128,144]{0,1:T(8,128)} %param.16) | copy-start | bytes 221188
  253.9 9.7 %copy-start.1 = (f32[128,2304]{1,0:T(8,128)}, f32[128,2304]{1,0:T(8,128)S(1)}, u32[]{:S(2)}) copy-start(f32[128,2304]{1,0:T(8,128)S(1)} %copy.35) | copy-start | bytes 3538948
  279.1 10.7 %copy-start.2 = (bf16[256,2048]{0,1:T(8,128)(2,1)S(1)}, bf16[256,2048]{0,1:T(8,128)(2,1)}, u32[]{:S(2)}) copy-start(bf16[256,2048]{0,1:T(8,128)(2,1)} %copy.55) | copy-start | bytes 3145732
Sparse Core Ops, SparseCore 0:
  12.1 187.6 all-reduce.1
Sparse Core Ops, SparseCore 1:
  12.9 62.5 all-gather.2
  78.4 84.6 reduce-scatter.1
where the time goes:
time: 311 us; the launch traced here: 310 us
  waiting for transfers between devices  173 us (56%)
  matrix products  50.2 us (16%)
  blocking collectives  48.4 us (16%)
  local copies, waits for them, and re-layouts  16.8 us (5%)
  between operations  15.7 us (5%)
  other arithmetic  6.63 us (2%)
    psum x1, waiting for transfers between devices, on_device(): lax.psum(own_delta.astype(jnp.bfloat16), 'rep').astype(jnp.float32)  172 us
    all_gather x1, blocking collectives, on_device(): lax.all_gather(momentum_new.astype(jnp.bfloat16), 'rep', axis=1, tiled=True)  48.4 us
    unnamed x24, local copies, waits for them, and re-layouts  12.5 us
    dot_general x1, matrix products, on_device(): jnp.einsum('grij,igrd->jgd', grad_scores, query_heads, preferred_element_...  8.69 us
    dot_general x1, matrix products, on_device(): jnp.einsum('grij,jgd->igrd', grad_scores, key_heads, preferred_element_ty...  7.65 us
    dot_general x1, matrix products, on_device(): jnp.dot(mixed_rows, full_weight, preferred_element_type=jnp.float32)  7.33 us
    dot_general x1, matrix products, on_device(): lax.dot_general(output_grad, full_weight, (((1,), (1,)), ((), ())), prefe...  7.28 us
  transfers between devices with their start and end apart: 3, of which 1 were waited for; matrix products, arithmetic and copies ran while one was open for 23% of the time, Pallas kernels for 0%

commit v1 on v0

--- a/solution.py
+++ b/solution.py
@@ -85,16 +85,20 @@
     grad_key = grad_key.reshape(length, KV_HEADS * HEAD_DIM).astype(jnp.bfloat16)
     grad_value = grad_value.reshape(length, KV_HEADS * HEAD_DIM).astype(jnp.bfloat16)
     replicas = lax.axis_size("rep")
-    position = lax.axis_index("rep")
     share_width = momentum.shape[1]
     own_delta = pseudo_grad[0]
-    mean_delta = lax.psum(own_delta.astype(jnp.bfloat16), "rep").astype(jnp.float32) / replicas
-    mean_share = lax.dynamic_slice_in_dim(mean_delta, position * share_width, share_width, 1)
+    rows = own_delta.shape[0]
+    shares = own_delta.astype(jnp.bfloat16).reshape(rows, replicas, share_width).transpose(1, 0, 2)
+    shares = lax.all_to_all(shares, "rep", 0, 0, tiled=False)
+    mean_share = jnp.sum(shares.astype(jnp.float32), axis=0) / replicas
     momentum_new = outer_moment * momentum + mean_share
-    momentum_full = lax.all_gather(
-        momentum_new.astype(jnp.bfloat16), "rep", axis=1, tiled=True
-    ).astype(momentum_new.dtype)
-    anchor_new = anchor - outer_rate * (outer_moment * momentum_full + mean_delta)
+    step_share = (outer_moment * momentum_new + mean_share).astype(jnp.bfloat16)
+    steps = lax.all_to_all(
+        jnp.broadcast_to(step_share[None], (replicas, rows, share_width)),
+        "rep", 0, 0, tiled=False,
+    )
+    step_full = steps.transpose(1, 0, 2).reshape(rows, replicas * share_width)
+    anchor_new = anchor - outer_rate * step_full.astype(jnp.float32)
     merged = (mix_factor * local_weight[0].astype(jnp.float32) + mix_factor * anchor_new).astype(
         jnp.bfloat16
     )[None]

time: 311 us -> 188 us (0.60)
  waiting for transfers between devices: 173 us -> 52.6 us
  blocking collectives: 48.4 us -> 36.2 us
  local copies, waits for them, and re-layouts: 16.8 us -> 22.6 us
  starting transfers between devices: 0.12 us -> 5.66 us
    psum x1 -> x0, waiting for transfers between devices: 172 us -> none  [on_device(): lax.psum(own_delta.astype(jnp.bfloat16), 'rep').astype(jnp.float32)]
    all_gather x1 -> x0, blocking collectives: 48.4 us -> none  [on_device(): lax.all_gather(momentum_new.astype(jnp.bfloat16), 'rep', axis=1, tiled=True)]
    all_to_all x0 -> x1, blocking collectives: none -> 36.2 us  [on_device(): shares = lax.all_to_all(shares, 'rep', 0, 0, tiled=False)]
    reduce_scatter x1, waiting for transfers between devices: 0.01 us -> 29.1 us  [on_device(): lax.psum_scatter(lax.dot_general(mixed_rows, output_grad, (((0,), (0,)),...]
    all_to_all x0 -> x1, waiting for transfers between devices: none -> 22.9 us  [on_device(): lax.all_to_all(jnp.broadcast_to(step_share[None], (replicas, rows, share_...]
    unnamed x24 -> x22, local copies, waits for them, and re-layouts: 12.5 us -> 18.2 us
    all_to_all x0 -> x1, starting transfers between devices: none -> 5.59 us  [on_device(): lax.all_to_all(jnp.broadcast_to(step_share[None], (replicas, rows, share_...]
  transfers between devices with their start and end apart: 3 -> 3, of which waited for: 1 -> 2; matrix products, arithmetic and copies ran while one was open for 23% -> 42% of each run, Pallas kernels for 0% -> 0%
where the time goes in v1:
time: 188 us; the launch traced here: 187 us
  waiting for transfers between devices  52.6 us (28%)
  matrix products  51.3 us (27%)
  blocking collectives  36.2 us (19%)
  local copies, waits for them, and re-layouts  22.6 us (12%)
  between operations  14.2 us (8%)
  starting transfers between devices  5.66 us (3%)
  other arithmetic  4.38 us (2%)
    all_to_all x1, blocking collectives, on_device(): shares = lax.all_to_all(shares, 'rep', 0, 0, tiled=False)  36.2 us
    reduce_scatter x1, waiting for transfers between devices, on_device(): lax.psum_scatter(lax.dot_general(mixed_rows, output_grad, (((0,), (0,)),...  29.1 us
    all_to_all x1, waiting for transfers between devices, on_device(): lax.all_to_all(jnp.broadcast_to(step_share[None], (replicas, rows, share_...  22.9 us
    unnamed x22, local copies, waits for them, and re-layouts  18.2 us
    dot_general x1, matrix products, on_device(): jnp.einsum('grij,igrd->jgd', grad_scores, query_heads, preferred_element_...  8.7 us
    dot_general x1, matrix products, on_device(): jnp.einsum('grij,jgd->igrd', grad_scores, key_heads, preferred_element_ty...  8.67 us
    dot_general x1, matrix products, on_device(): jnp.dot(mixed_rows, full_weight, preferred_element_type=jnp.float32)  7.51 us
    dot_general x1, matrix products, on_device(): lax.dot_general(output_grad, full_weight, (((1,), (1,)), ((), ())), prefe...  7.28 us
  transfers between devices with their start and end apart: 3, of which 2 were waited for; matrix products, arithmetic and copies ran while one was open for 42% of the time, Pallas kernels for 0%

profile of v1, /device:TPU:8, one launch (start us, length us, event | category | flops | bytes accessed | tf_op | source)
XLA Modules:
  0.0 186.9 jit_solution(7425592715676645031)
XLA Ops:
  9.1 1.3 copy.74
  10.8 1.7 copy.71
  12.5 3.5 %fusion.42 = (f32[8,2,256]{2,1,0:T(2,128)S(1)}, f32[8,2,256,256]{2,3,1,0:T(8,128)}) fusion(pred[256,256]{0,1:T(8,128)(4,1)S(1)} %iota_compare_fusion, bf16[256,8,128,1]{0,2,3,1:T(8,128)(2,1)S(1)} %copy.58, bf16[256,8,2,128]{0,3,2,1:T(8,128)(2,1)S(1)} %bitcast.120), kind=kOutput, calls=%fused_computation.52 | convolution fusion | flops 272630016 | bytes 5849088 | tf_op jit(solution)/shard_map/sub | solution.py:26
  16.1 2.8 %convolution_convert_fusion.1 = bf16[8,2,256,128]{2,3,1,0:T(8,128)(2,1)S(1)} fusion(bf16[256,8,128,1]{2,1,0,3:T(8,128)(2,1)S(1)} %bitcast.118, f32[8,2,256,256]{2,3,1,0:T(8,128)} %get-tuple-element.29, f32[8,2,256]{2,1,0:T(2,128)S(1)} %get-tuple-element.28), kind=kOutput, calls=%fused_computation.24 | convolution fusion | flops 271056896 | bytes 5783552 | tf_op jit(solution)/shard_map/grij,jgd->igrd/dot_general | solution.py:48
  18.9 5.1 %convolution_convert_fusion = bf16[2048,2304]{1,0:T(8,128)(2,1)} fusion(bf16[256,2048]{0,1:T(8,128)(2,1)S(1)} %bitcast.112, bf16[256,2304]{1,0:T(8,128)(2,1)S(1)} %copy-done), kind=kOutput, calls=%fused_computation.2 | convolution fusion | flops 2420637696 | bytes 11665408 | tf_op jit(solution)/shard_map/dot_general | solution.py:61
  24.0 1.9 %copy.45 = bf16[1,128,2304]{1,2,0:T(8,128)(2,1)S(1)} copy(f32[1,128,2304]{2,1,0:T(8,128)} %param.14) | data formatting | bytes 1769472 | tf_op args[5]
  25.9 36.2 %all_to_all.10 = bf16[16,128,144]{1,2,0:T(8,128)(2,1)S(1)} all-to-all(bf16[16,128,144]{1,2,0:T(8,128)(2,1)S(1)} %bitcast.116), channel_id=1, replica_groups=mesh['rep'=16,'fsdp'=16] {'rep'}, dimensions={0} | all-to-all | bytes 1179648 | tf_op jit(solution)/shard_map/all_to_all | solution.py:92
  63.7 5.6 %all-to-all-start.1 = ((bf16[16,128,144]{1,2,0:T(8,128)(2,1)}), bf16[16,128,144]{1,2,0:T(8,128)(2,1)}, u32[]{:S(2)}, u32[]{:S(2)}) async-start(bf16[16,128,144]{1,2,0:T(8,128)(2,1)} %broadcast_in_dim.28), calls=%async_computation.2 | async-start | bytes 1179648 | tf_op jit(solution)/shard_map/all_to_all | solution.py:96
  70.4 1.6 copy.46
  72.0 22.9 %all-to-all-done.1 = bf16[16,128,144]{1,2,0:T(8,128)(2,1)} async-done(((bf16[16,128,144]{1,2,0:T(8,128)(2,1)}), bf16[16,128,144]{1,2,0:T(8,128)(2,1)}, u32[]{:S(2)}, u32[]{:S(2)}) %all-to-all-start.1) | async-done | bytes 589856 | tf_op jit(solution)/shard_map/all_to_all | solution.py:96
  96.0 2.5 %fusion.30 = (bf16[1,128,2304]{1,2,0:T(8,128)(2,1)}, f32[128,2304]{0,1:T(8,128)}) fusion(bf16[1,128,2304]{1,2,0:T(8,128)(2,1)} %copy.47, f32[128,2304]{0,1:T(8,128)S(1)} %copy.46, f32[16,128,144]{1,2,0:T(8,128)S(1)} %convert_multiply_fusion), kind=kLoop, calls=%fused_computation.38 | loop fusion | flops 1474560 | bytes 4718592 | tf_op jit(solution)/shard_map/broadcast_in_dim | solution.py:102
  98.5 2.7 %copy.51 = f32[128,2304]{1,0:T(8,128)} copy(f32[128,2304]{0,1:T(8,128)} %get-tuple-element.25) | data formatting | bytes 2359296
  101.1 2.1 %copy.52 = bf16[1,128,2304]{2,1,0:T(8,128)(2,1)} copy(bf16[1,128,2304]{1,2,0:T(8,128)(2,1)} %get-tuple-element.24) | data formatting | bytes 1179648
  103.3 7.3 %fusion.13 = bf16[256,2048]{1,0:T(8,128)(2,1)} fusion(bf16[256,2304]{1,0:T(8,128)(2,1)S(1)} %copy-done, bf16[1,2048,2304]{2,1,0:T(8,128)(2,1)} %all-gather.3.cloned.1.call-done), kind=kOutput, calls=%fused_computation.16 | convolution fusion | flops 2416443392 | bytes 11665408 | tf_op jit(solution)/shard_map/dot_general | solution.py:55
  110.5 1.5 copy.72
  112.0 3.8 %fusion.32 = f32[8,256,2,256]{1,3,2,0:T(8,128)} fusion(bf16[256,8,2,128]{0,3,2,1:T(8,128)(2,1)S(1)} %bitcast.114, bf16[256,8,128,1]{2,1,0,3:T(8,128)(2,1)} %bitcast.119), kind=kOutput, calls=%fused_computation.40 | convolution fusion | flops 268435456 | bytes 5767168 | tf_op jit(solution)/shard_map/igrd,jgd->grij/dot_general | solution.py:70
  115.9 8.7 %fusion.22 = bf16[8,2,256,128]{2,3,1,0:T(8,128)(2,1)} fusion(bf16[256,8,128,1]{0,2,3,1:T(8,128)(2,1)} %copy-done.4, f32[8,256,2,256]{1,3,2,0:T(8,128)} %fusion.32, f32[8,2,256,256]{2,3,1,0:T(8,128)} %get-tuple-element.29, f32[8,2,256]{2,1,0:T(2,128)S(1)} %get-tuple-element.28), kind=kOutput, calls=%fused_computation.25 | convolution fusion | flops 276304128 | bytes 9977856 | tf_op jit(solution)/shard_map/grij,jgd->igrd/dot_general | solution.py:75
  124.5 2.3 %copy.48 = bf16[256,2048]{1,0:T(8,128)(2,1)} copy(bf16[256,2048]{0,1:T(8,128)(2,1)} %bitcast.122) | data formatting | bytes 2097152
  126.8 8.7 %fusion.25 = bf16[8,256,128]{1,2,0:T(8,128)(2,1)} fusion(bf16[256,8,2,128]{0,3,2,1:T(8,128)(2,1)} %bitcast.121, f32[8,256,2,256]{1,3,2,0:T(8,128)} %fusion.32, f32[8,2,256,256]{2,3,1,0:T(8,128)} %get-tuple-element.29, f32[8,2,256]{2,1,0:T(2,128)S(1)} %get-tuple-element.28), kind=kOutput, calls=%fused_computation.29 | convolution fusion | flops 276041984 | bytes 9977856 | tf_op jit(solution)/shard_map/grij,igrd->jgd/dot_general | solution.py:78
  135.5 2.0 %copy.49 = bf16[256,1024]{1,0:T(8,128)(2,1)} copy(bf16[256,1024]{0,1:T(8,128)(2,1)} %bitcast.126) | data formatting | bytes 1048576
  137.5 3.9 %fusion.24 = bf16[8,128,256]{2,1,0:T(8,128)(2,1)} fusion(bf16[256,8,2,128]{0,3,2,1:T(8,128)(2,1)S(1)} %bitcast.115, f32[8,2,256,256]{2,3,1,0:T(8,128)} %get-tuple-element.29, f32[8,2,256]{2,1,0:T(2,128)S(1)} %get-tuple-element.28), kind=kOutput, calls=%fused_computation.28 | convolution fusion | flops 270794752 | bytes 5783552 | tf_op jit(solution)/shard_map/grij,igrd->jgd/dot_general | solution.py:81
  141.5 2.0 %copy.50 = bf16[256,1024]{1,0:T(8,128)(2,1)} copy(bf16[256,1024]{0,1:T(8,128)(2,1)} %bitcast.125) | data formatting | bytes 1048576
  143.5 7.5 %fusion.9 = bf16[256,2304]{1,0:T(8,128)(2,1)} fusion(bf16[256,2048]{0,1:T(8,128)(2,1)S(1)} %bitcast.113, bf16[1,2048,2304]{2,1,0:T(8,128)(2,1)} %all-gather.3.cloned.1.call-done), kind=kOutput, calls=%fused_computation.14 | convolution fusion | flops 2416508928 | bytes 11665408 | tf_op jit(solution)/shard_map/dot_general | solution.py:54
  151.0 29.1 %reduce-scatter.2.cloned.1.call-done = bf16[128,2304]{1,0:T(8,128)(2,1)} async-done(((bf16[2048,2304]{1,0:T(8,128)(2,1)}), bf16[128,2304]{1,0:T(8,128)(2,1)}) %reduce-scatter.2.cloned.1.call-update) | async-done | bytes 589840 | tf_op jit(solution)/shard_map/reduce_scatter | solution.py:60
  (25 shorter events, 6.1 us)
Async XLA Ops:
  7.2 11.7 %copy-start = (bf16[256,2304]{1,0:T(8,128)(2,1)S(1)}, bf16[256,2304]{1,0:T(8,128)(2,1)}, u32[]{:S(2)}) copy-start(bf16[256,2304]{1,0:T(8,128)(2,1)} %param.12) | copy-start | bytes 3538948
  7.2 96.1 %all-gather.3.cloned.1.call-start = ((), (), s32[]{:S(2)}) async-start(), calls=%async_computation.4 | async-start | bytes 10027008 | tf_op jit(solution)/shard_map/all_gather | solution.py:53
  7.9 172.2 %reduce-scatter.2.cloned.1.call-start = ((), (), s32[]{:S(2)}) async-start(), calls=%async_computation.3 | async-start | bytes 10027008 | tf_op jit(solution)/shard_map/reduce_scatter | solution.py:60
  9.1 6.9 %copy-start.1 = (bf16[32,8,8,128]{3,2,1,0:T(8,128)(2,1)}, bf16[32,8,8,128]{3,2,1,0:T(8,128)(2,1)S(1)}, u32[]{:S(2)}) copy-start(bf16[32,8,8,128]{3,2,1,0:T(8,128)(2,1)S(1)} %copy.73) | copy-start | bytes 1572868
  10.8 5.3 %copy-start.4 = (bf16[256,8,128,1]{0,2,3,1:T(8,128)(2,1)}, bf16[256,8,128,1]{0,2,3,1:T(8,128)(2,1)S(1)}, u32[]{:S(2)}) copy-start(bf16[256,8,128,1]{0,2,3,1:T(8,128)(2,1)S(1)} %copy.58) | copy-start | bytes 1572868
  12.5 3.6 %copy-start.2 = (bf16[256,2048]{0,1:T(8,128)(2,1)}, bf16[256,2048]{0,1:T(8,128)(2,1)S(1)}, u32[]{:S(2)}) copy-start(bf16[256,2048]{0,1:T(8,128)(2,1)S(1)} %copy.71) | copy-start | bytes 3145732
  23.9 38.2 %copy-start.5 = (f32[128,144]{0,1:T(8,128)S(1)}, f32[128,144]{0,1:T(8,128)}, u32[]{:S(2)}) copy-start(f32[128,144]{0,1:T(8,128)} %param.16) | copy-start | bytes 221188
  24.0 45.3 %copy-start.3 = (bf16[1,128,2304]{2,1,0:T(8,128)(2,1)S(1)}, bf16[1,128,2304]{2,1,0:T(8,128)(2,1)}, u32[]{:S(2)}) copy-start(bf16[1,128,2304]{2,1,0:T(8,128)(2,1)} %param.17) | copy-start | bytes 1769476
  63.7 31.2 %all-to-all-start.1 = ((bf16[16,128,144]{1,2,0:T(8,128)(2,1)}), bf16[16,128,144]{1,2,0:T(8,128)(2,1)}, u32[]{:S(2)}, u32[]{:S(2)}) async-start(bf16[16,128,144]{1,2,0:T(8,128)(2,1)} %broadcast_in_dim.28), calls=%async_computation.2 | async-start | bytes 1179648 | tf_op jit(solution)/shard_map/all_to_all | solution.py:96
Sparse Core Ops, SparseCore 0:
  9.9 87.8 all-gather.2
  100.8 79.1 reduce-scatter.1

commit v2 on v0

v2 whole, which is shorter than its diff:
```python
import math

import jax
import jax.numpy as jnp
from jax import lax
from jax.experimental import pallas as pl
from jax.experimental.pallas import tpu as pltpu
from jax.sharding import PartitionSpec as P

HEADS = 16
KV_HEADS = 8
HEAD_DIM = 128

query_scale = 1.0 / 12.0
outer_rate = 0.7
outer_moment = 0.9
mix_factor = 0.5

X_SIZE = 4
Z_SIZE = 2
VMEM_LIMIT = 56 * 1024 * 1024

NT = (((1,), (1,)), ((), ()))
TN = (((0,), (0,)), ((), ()))


def f32_dot(left, right, dims=(((1,), (0,)), ((), ()))):
    return lax.dot_general(left, right, dims, preferred_element_type=jnp.float32)


def params(**kwargs):
    return pltpu.CompilerParams(vmem_limit_bytes=VMEM_LIMIT, **kwargs)


def cost(microseconds, bytes_accessed):
    return pl.CostEstimate(
        flops=int(microseconds * 1.15e9), bytes_accessed=bytes_accessed, transcendentals=0
    )


def own_lanes(place_ref, turn):
    parity = place_ref[KV_HEADS] if turn == 0 else 1 - place_ref[KV_HEADS]
    return pl.ds(pl.multiple_of(parity * HEAD_DIM, HEAD_DIM), HEAD_DIM)


def forward_kernel(place_ref, q_ref, k_ref, v_ref, own_ref, other_ref, attention_ref):
    length = q_ref.shape[0]
    keys, values = k_ref[...], v_ref[...]
    allowed = lax.broadcasted_iota(jnp.int32, (length, length), 0) >= lax.broadcasted_iota(
        jnp.int32, (length, length), 1
    )
    for turn, out_ref in enumerate((own_ref, other_ref)):
        scores = f32_dot(q_ref[:, own_lanes(place_ref, turn)], keys, NT)
        scores = jnp.where(allowed, scores, -jnp.inf)
        highest = jnp.max(scores, axis=-1, keepdims=True)
        terms = jnp.exp2((scores - highest) * (query_scale * math.log2(math.e)))
        attention = terms * (1.0 / jnp.sum(terms, axis=-1, keepdims=True))
        attention_ref[0, turn] = attention
        out_ref[...] = f32_dot(attention.astype(jnp.bfloat16), values).astype(jnp.bfloat16)


def forward(place, query_states, key_states, value_states):
    length = query_states.shape[0]
    pair = 2 * HEAD_DIM
    half = KV_HEADS * HEAD_DIM
    kv_spec = pl.BlockSpec((length, HEAD_DIM), lambda r, place: (0, place[r]))
    out_spec = pl.BlockSpec((length, HEAD_DIM), lambda r, place: (0, r))
    return pl.pallas_call(
        forward_kernel,
        grid_spec=pltpu.PrefetchScalarGridSpec(
            num_scalar_prefetch=1,
            grid=(KV_HEADS,),
            in_specs=[
                pl.BlockSpec((length, pair), lambda r, place: (0, place[r])),
                kv_spec,
                kv_spec,
            ],
            out_specs=[
                out_spec,
                out_spec,
                pl.BlockSpec((1, 2, length, length), lambda r, place: (r, 0, 0, 0)),
            ],
        ),
        out_shape=[
            jax.ShapeDtypeStruct((length, half), jnp.bfloat16),
            jax.ShapeDtypeStruct((length, half), jnp.bfloat16),
            jax.ShapeDtypeStruct((KV_HEADS, 2, length, length), jnp.float32),
        ],
        compiler_params=params(),
        cost_estimate=cost(9, 8 * 2**20),
        name="attention_forward",
    )(place, query_states, key_states, value_states)


def backward_kernel(
    place_ref, q_ref, k_ref, v_ref, attention_ref, own_ref, other_ref, dq_ref, dk_ref, dv_ref
):
    keys, values = k_ref[...], v_ref[...]
    for turn, grad_ref in enumerate((own_ref, other_ref)):
        lanes = own_lanes(place_ref, turn)
        grad_mixed = grad_ref[...]
        attention = attention_ref[0, turn]
        grad_probs = f32_dot(grad_mixed, values, NT)
        row_term = jnp.sum(attention * grad_probs, axis=-1, keepdims=True)
        grad_scores = (attention * (grad_probs - row_term) * query_scale).astype(jnp.bfloat16)
        dq_ref[:, lanes] = f32_dot(grad_scores, keys).astype(jnp.bfloat16)
        dk = f32_dot(grad_scores, q_ref[:, lanes], TN)
        dv = f32_dot(attention.astype(jnp.bfloat16), grad_mixed, TN)
        if turn == 0:
            dk_sum, dv_sum = dk, dv
    dk_ref[...] = (dk_sum + dk).astype(jnp.bfloat16)
    dv_ref[...] = (dv_sum + dv).astype(jnp.bfloat16)


def backward(place, query_states, key_states, value_states, attention, grad_own, grad_other):
    length = query_states.shape[0]
    pair = 2 * HEAD_DIM
    pair_spec = pl.BlockSpec((length, pair), lambda r, place: (0, place[r]))
    kv_spec = pl.BlockSpec((length, HEAD_DIM), lambda r, place: (0, place[r]))
    slot_spec = pl.BlockSpec((length, HEAD_DIM), lambda r, place: (0, r))
    return pl.pallas_call(
        backward_kernel,
        grid_spec=pltpu.PrefetchScalarGridSpec(
            num_scalar_prefetch=1,
            grid=(KV_HEADS,),
            in_specs=[
                pair_spec,
                kv_spec,
                kv_spec,
                pl.BlockSpec((1, 2, length, length), lambda r, place: (r, 0, 0, 0)),
                slot_spec,
                slot_spec,
            ],
            out_specs=[pair_spec, kv_spec, kv_spec],
        ),
        out_shape=[
            jax.ShapeDtypeStruct(query_states.shape, jnp.bfloat16),
            jax.ShapeDtypeStruct(key_states.shape, jnp.bfloat16),
            jax.ShapeDtypeStruct(value_states.shape, jnp.bfloat16),
        ],
        compiler_params=params(),
        cost_estimate=cost(10, 9 * 2**20),
        name="attention_backward",
    )(place, query_states, key_states, value_states, attention, grad_own, grad_other)


COLUMN_TILES = 3


def weight_grad_kernel(splits, m0_ref, m1_ref, g0_ref, g1_ref, *out_refs):
    product = f32_dot(m0_ref[...], g0_ref[...], TN) + f32_dot(m1_ref[...], g1_ref[...], TN)
    product = product.astype(jnp.bfloat16)
    start = 0
    for rows, out_ref in zip(splits, out_refs):
        out_ref[...] = product[start : start + rows]
        start += rows


def weight_grad_pieces(mixed_own, mixed_peer, grad_own, grad_peer, splits):
    length, half = mixed_own.shape
    width = grad_own.shape[1]
    tile = width // COLUMN_TILES
    whole = pl.BlockSpec((length, half), lambda j: (0, 0))
    part = pl.BlockSpec((length, tile), lambda j: (0, j))
    return pl.pallas_call(
        lambda *refs: weight_grad_kernel(splits, *refs),
        grid=(COLUMN_TILES,),
        in_specs=[whole, whole, part, part],
        out_specs=[pl.BlockSpec((rows, tile), lambda j: (0, j)) for rows in splits],
        out_shape=[jax.ShapeDtypeStruct((rows, width), jnp.bfloat16) for rows in splits],
        compiler_params=params(),
        cost_estimate=cost(5, 8 * 2**20),
        name="weight_grad_partial",
    )(mixed_own, mixed_peer, grad_own, grad_peer)


def grad_mixed_kernel(g0_ref, g1_ref, *refs):
    *pieces, out0_ref, out1_ref, sum0, sum1 = refs
    step = pl.program_id(0)
    weight = jnp.concatenate([piece[...] for piece in pieces], axis=0)
    part0 = f32_dot(g0_ref[...], weight, NT)
    part1 = f32_dot(g1_ref[...], weight, NT)

    @pl.when(step == 0)
    def _():
        sum0[...] = part0
        sum1[...] = part1

    @pl.when(step > 0)
    def _():
        sum0[...] += part0
        sum1[...] += part1

    @pl.when(step == COLUMN_TILES - 1)
    def _():
        out0_ref[...] = sum0[...].astype(jnp.bfloat16)
        out1_ref[...] = sum1[...].astype(jnp.bfloat16)


def grad_mixed_of(grad_own, grad_peer, pieces):
    length, width = grad_own.shape
    tile = width // COLUMN_TILES
    out_width = sum(piece.shape[0] for piece in pieces)
    part = pl.BlockSpec((length, tile), lambda j: (0, j))
    out_spec = pl.BlockSpec((length, out_width), lambda j: (0, 0))
    out = jax.ShapeDtypeStruct((length, out_width), jnp.bfloat16)
    return pl.pallas_call(
        grad_mixed_kernel,
        grid=(COLUMN_TILES,),
        in_specs=[part, part]
        + [pl.BlockSpec((piece.shape[0], tile), lambda j: (0, j)) for piece in pieces],
        out_specs=[out_spec, out_spec],
        out_shape=[out, out],
        scratch_shapes=[pltpu.VMEM((length, out_width), jnp.float32)] * 2,
        compiler_params=params(),
        cost_estimate=cost(6, 8 * 2**20),
        name="grad_mixed",
    )(grad_own, grad_peer, *pieces)


def branch_kernel(addends, mixed_ref, *refs):
    *pieces, out_ref = refs
    added, pieces = pieces[:addends], pieces[addends:]
    weight = jnp.concatenate([piece[...] for piece in pieces], axis=0)
    product = f32_dot(mixed_ref[...], weight)
    for ref in added:
        product = product + ref[...].astype(jnp.float32)
    out_ref[...] = product.astype(jnp.bfloat16)


def branch_part(mixed, pieces, *addends):
    length, half = mixed.shape
    width = pieces[0].shape[1]
    tile = width // COLUMN_TILES
    part = pl.BlockSpec((length, tile), lambda j: (0, j))
    return pl.pallas_call(
        lambda *refs: branch_kernel(len(addends), *refs),
        grid=(COLUMN_TILES,),
        in_specs=[pl.BlockSpec((length, half), lambda j: (0, 0))]
        + [part] * len(addends)
        + [pl.BlockSpec((piece.shape[0], tile), lambda j: (0, j)) for piece in pieces],
        out_specs=part,
        out_shape=jax.ShapeDtypeStruct((length, width), jnp.bfloat16),
        compiler_params=params(),
        cost_estimate=cost(5, 8 * 2**20),
        name="branch",
    )(mixed, *addends, *pieces)


def shift(dz, dx, dcore):
    pairs = []
    for z in range(Z_SIZE):
        for x in range(X_SIZE):
            for core in range(2):
                target = ((z + dz) % Z_SIZE) * X_SIZE + (x + dx) % X_SIZE
                pairs.append(((z * X_SIZE + x) * 2 + core, target * 2 + (core + dcore) % 2))
    return pairs


def to_right(array):
    return lax.ppermute(array, "fsdp", shift(0, 1, 0))


def to_left(array):
    return lax.ppermute(array, "fsdp", shift(0, -1, 0))


def to_far(array):
    return lax.ppermute(array, "fsdp", shift(1, 0, 0))


def to_peer(array):
    return lax.ppermute(array, "fsdp", shift(0, 0, 1))


def added(*terms):
    total = terms[0].astype(jnp.float32)
    for term in terms[1:]:
        total = total + term.astype(jnp.float32)
    return total.astype(jnp.bfloat16)


def place_table():
    position = lax.axis_index("fsdp")
    z, x, core = position // (2 * X_SIZE), (position // 2) % X_SIZE, position % 2
    slots = jnp.arange(KV_HEADS, dtype=jnp.int32)
    heads = ((z + slots // X_SIZE) % Z_SIZE) * X_SIZE + (x + slots % X_SIZE) % X_SIZE
    return jnp.concatenate([heads, core[None]]).astype(jnp.int32)


def outer_update(own_delta, anchor, momentum, local):
    replicas = lax.axis_size("rep")
    rows, share_width = momentum.shape
    shares = own_delta.astype(jnp.bfloat16).reshape(rows, replicas, share_width)
    shares = lax.all_to_all(shares.transpose(1, 2, 0), "rep", 0, 0, tiled=False)
    mean_share = jnp.sum(shares.astype(jnp.float32), axis=0).T / replicas
    momentum_new = outer_moment * momentum + mean_share
    step_share = (outer_moment * momentum_new + mean_share).astype(jnp.bfloat16).T
    steps = jnp.broadcast_to(step_share[None], (replicas, share_width, rows))
    steps = lax.all_to_all(steps, "rep", 0, 0, tiled=False)
    step_full = steps.reshape(replicas * share_width, rows).T
    anchor_new = anchor - outer_rate * step_full.astype(jnp.float32)
    merged = mix_factor * local.astype(jnp.float32) + mix_factor * anchor_new
    return momentum_new, anchor_new, merged.astype(jnp.bfloat16)


def on_device(
    query_states,
    key_states,
    value_states,
    output_grad,
    out_weight,
    pseudo_grad,
    anchor,
    momentum,
    local_weight,
):
    place = place_table()
    own_rows = out_weight[0]
    half = own_rows.shape[0] // 2
    grad_peer = to_peer(output_grad)

    w3 = to_right(own_rows)
    w1 = to_left(own_rows)
    w4 = to_far(own_rows)
    mixed_own, mixed_other, attention = forward(place, query_states, key_states, value_states)
    mixed_peer = to_peer(mixed_other)
    w1, w3, w4, mixed_own = lax.optimization_barrier((w1, w3, w4, mixed_own))
    w2a = to_right(w3[:half])
    w2b = to_left(w1[half:])
    w7 = to_right(w4)
    w5 = to_left(w4)

    rows = [2 * half, 2 * half, half, half, 2 * half, 2 * half, 2 * half, 2 * half, 2 * half]
    d0, d1, d2a, d2b, d3, d4, d5, d6, d7 = weight_grad_pieces(
        mixed_own, mixed_peer, output_grad, grad_peer, rows
    )
    w2a, w2b, d6 = lax.optimization_barrier((w2a, w2b, d6))
    w6a = to_far(w2a)
    w6b = to_far(w2b)
    pieces = [own_rows, w1, w2a, w2b, w3, w4, w5, w6a, w6b, w7]
    top, bottom = ((0, half), (0, 0)), ((half, 0), (0, 0))
    r2 = to_far(d6)
    r4l = to_left(d7)
    r4r = to_right(d5)
    from_far = to_far(added(d4, r4l, r4r))
    r3a = to_left(added(d2a, r2[:half]))
    r1b = to_right(added(d2b, r2[half:]))
    from_right = to_left(added(d3, jnp.pad(r3a, top)))
    from_left = to_right(added(d1, jnp.pad(r1b, bottom)))
    weight_grad = added(d0, from_right, from_left, from_far)[None]

    grad_mixed, grad_send = grad_mixed_of(output_grad, grad_peer, pieces)
    grad_mixed_other = to_peer(grad_send)
    branch_peer = to_peer(branch_part(mixed_peer, pieces))
    grad_query, grad_key, grad_value = backward(
        place, query_states, key_states, value_states, attention, grad_mixed, grad_mixed_other
    )
    branch_out = branch_part(mixed_own, pieces, branch_peer)

    momentum_new, anchor_new, merged = outer_update(
        pseudo_grad[0], anchor, momentum, local_weight[0]
    )
    return (
        branch_out,
        grad_query,
        grad_key,
        grad_value,
        weight_grad,
        anchor_new,
        momentum_new,
        merged[None],
    )


def solution(mesh):
    return jax.shard_map(
        on_device,
        mesh=mesh,
        in_specs=(
            P(("rep", "fsdp"), None),
            P(("rep", "fsdp"), None),
            P(("rep", "fsdp"), None),
            P(("rep", "fsdp"), None),
            P("rep", "fsdp", None),
            P("rep", "fsdp", None),
            P("fsdp", None),
            P("fsdp", "rep"),
            P("rep", "fsdp", None),
        ),
        out_specs=(
            P(("rep", "fsdp"), None),
            P(("rep", "fsdp"), None),
            P(("rep", "fsdp"), None),
            P(("rep", "fsdp"), None),
            P("rep", "fsdp", None),
            P("fsdp", None),
            P("fsdp", "rep"),
            P("rep", "fsdp", None),
        ),
        check_vma=False,
    )
```

time: 311 us -> 134 us (0.43)
  waiting for transfers between devices: 173 us -> 23.8 us
  matrix products: 50.2 us -> 0 us
  blocking collectives: 48.4 us -> 0 us
  Pallas kernels: 0 us -> 45.8 us
  starting transfers between devices: 0.12 us -> 45.6 us
  between operations: 15.7 us -> 0.83 us
  local copies, waits for them, and re-layouts: 16.8 us -> 9.83 us
    psum x1 -> x0, waiting for transfers between devices: 172 us -> none  [on_device(): lax.psum(own_delta.astype(jnp.bfloat16), 'rep').astype(jnp.float32)]
    all_gather x1 -> x0, blocking collectives: 48.4 us -> none  [on_device(): lax.all_gather(momentum_new.astype(jnp.bfloat16), 'rep', axis=1, tiled=True)]
    dot_general x8 -> x0, matrix products: 46.7 us -> none  [the longest x1 8.69 us: on_device(): jnp.einsum('grij,igrd->jgd', grad_scores, query_heads, preferred_element_...]
    pallas_call x0 -> x6, Pallas kernels: none -> 45.8 us  [the longest x2 11.6 us: branch_part(): pl.pallas_call(lambda *refs: branch_kernel(len(addends), *refs), grid=(CO...]
    ppermute x0 -> x21, starting transfers between devices: none -> 25.3 us  [the longest x6 17.8 us: to_left(): return lax.ppermute(array, 'fsdp', shift(0, -1, 0))]
    ppermute x0 -> x21, waiting for transfers between devices: none -> 23.8 us  [the longest x6 12.9 us: to_right(): return lax.ppermute(array, 'fsdp', shift(0, 1, 0))]
    all_to_all x0 -> x2, starting transfers between devices: none -> 20.3 us  [the longest x1 10.7 us: outer_update(): shares = lax.all_to_all(shares.transpose(1, 2, 0), 'rep', 0, 0, tiled=False)]
    unnamed x24 -> x29, local copies, waits for them, and re-layouts: 12.5 us -> 6.95 us
  transfers between devices with their start and end apart: 3 -> 23, of which waited for: 1 -> 5; matrix products, arithmetic and copies ran while one was open for 23% -> 10% of each run, Pallas kernels for 0% -> 34%
where the time goes in v2:
time: 134 us; the launch traced here: 133 us
  Pallas kernels  45.8 us (34%)
  starting transfers between devices  45.6 us (34%)
  waiting for transfers between devices  23.8 us (18%)
  local copies, waits for them, and re-layouts  9.83 us (7%)
  other arithmetic  7.17 us (5%)
    ppermute x6, starting transfers between devices, to_left(): return lax.ppermute(array, 'fsdp', shift(0, -1, 0))  17.8 us
    ppermute x6, waiting for transfers between devices, to_right(): return lax.ppermute(array, 'fsdp', shift(0, 1, 0))  12.9 us
    pallas_call x2, Pallas kernels, branch_part(): pl.pallas_call(lambda *refs: branch_kernel(len(addends), *refs), grid=(CO...  11.6 us
    pallas_call x1, Pallas kernels, forward(): pl.pallas_call(forward_kernel, grid_spec=pltpu.PrefetchScalarGridSpec(num...  10.8 us
    pallas_call x1, Pallas kernels, backward(): pl.pallas_call(backward_kernel, grid_spec=pltpu.PrefetchScalarGridSpec(nu...  10.7 us
    all_to_all x1, starting transfers between devices, outer_update(): shares = lax.all_to_all(shares.transpose(1, 2, 0), 'rep', 0, 0, tiled=False)  10.7 us
    ppermute x5, waiting for transfers between devices, to_far(): return lax.ppermute(array, 'fsdp', shift(1, 0, 0))  9.77 us
    all_to_all x1, starting transfers between devices, outer_update(): steps = lax.all_to_all(steps, 'rep', 0, 0, tiled=False)  9.63 us
  transfers between devices with their start and end apart: 23, of which 5 were waited for; matrix products, arithmetic and copies ran while one was open for 10% of the time, Pallas kernels for 34%

profile of v2, /device:TPU:8, one launch (start us, length us, event | category | flops | bytes accessed | tf_op | source)
XLA Modules:
  0.0 133.0 jit_solution(9802075024484970770)
XLA Ops:
  0.6 2.8 %collective-permute-start = (bf16[128,2304]{1,0:T(8,128)(2,1)}, bf16[128,2304]{1,0:T(8,128)(2,1)}, u32[]{:S(2)}, u32[]{:S(2)}) collective-permute-start(bf16[128,2304]{1,0:T(8,128)(2,1)} %bitcast.27), channel_id=1, source_target_pairs={{0,6},{1,7},{2,0},{3,1},{4,2},{5,3},{6,4},{7,5},{8,14},{9,15},{10,... | collective-permute-start | bytes 1769480 | tf_op jit(solution)/shard_map/ppermute | solution.py:265
  3.5 1.9 %collective-permute-start.2 = (bf16[128,2304]{1,0:T(8,128)(2,1)}, bf16[128,2304]{1,0:T(8,128)(2,1)}, u32[]{:S(2)}, u32[]{:S(2)}) collective-permute-start(bf16[128,2304]{1,0:T(8,128)(2,1)} %bitcast.29), channel_id=1, source_target_pairs={{0,8},{1,9},{2,10},{3,11},{4,12},{5,13},{6,14},{7,15},{8,0},{9,1},... | collective-permute-start | bytes 1769480 | tf_op jit(solution)/shard_map/ppermute | solution.py:269
  5.4 2.3 %copy.18 = bf16[1,128,2304]{1,2,0:T(8,128)(2,1)} copy(f32[1,128,2304]{2,1,0:T(8,128)} %param.14) | data formatting | bytes 1769472 | tf_op args[5]
  7.7 10.7 %all-to-all-start = ((bf16[16,144,128]{2,1,0:T(8,128)(2,1)}), bf16[16,144,128]{2,1,0:T(8,128)(2,1)S(1)}, u32[]{:S(2)}, u32[]{:S(2)}) async-start(bf16[16,144,128]{2,1,0:T(8,128)(2,1)} %bitcast.4), calls=%async_computation | async-start | bytes 1179648 | tf_op jit(solution)/shard_map/all_to_all | solution.py:295
  19.0 10.8 %attention_forward.1 = (bf16[256,1024]{1,0:T(8,128)(2,1)}, bf16[256,1024]{1,0:T(8,128)(2,1)}, f32[8,2,256,256]{3,2,1,0:T(8,128)}) custom-call(s32[9]{0:T(128)} %pad_add_fusion.place_ref, bf16[256,2048]{1,0:T(8,128)(2,1)} %q_ref.3, bf16[256,1024]{1,0:T(8,128)(2,1)} %k_ref.3, bf16[256,1024]{1,0:T(8,128)(2,1)} %v_ref.3), custom_call_target="tpu_custom_call" | custom-call | flops 10350000128 | bytes 8388608 | tf_op jit(solution)/shard_map/attention_forward/pallas_call | solution.py:68
  32.0 2.6 %collective-permute-start.7 = (bf16[128,2304]{1,0:T(8,128)(2,1)}, bf16[128,2304]{1,0:T(8,128)(2,1)}, u32[]{:S(2)}, u32[]{:S(2)}) collective-permute-start(bf16[128,2304]{1,0:T(8,128)(2,1)} %collective-permute-done.2.refs_6_.refs_7_.refs_5_), channel_id=1, source_target_pairs={{0,6},{1,7},{2,0},{3,1},{4,2},{5,3},{6,4},{7,5},{8,14},{9,15},{10,... | collective-permute-start | bytes 1769480 | tf_op jit(solution)/shard_map/ppermute | solution.py:265
  36.7 3.3 %collective-permute-start.5 = (bf16[64,2304]{1,0:T(8,128)(2,1)S(1)}, bf16[64,2304]{1,0:T(8,128)(2,1)}, u32[]{:S(2)}, u32[]{:S(2)}) collective-permute-start(bf16[64,2304]{1,0:T(8,128)(2,1)S(1)} %slice.13), channel_id=1, source_target_pairs={{0,6},{1,7},{2,0},{3,1},{4,2},{5,3},{6,4},{7,5},{8,14},{9,15},{10,... | collective-permute-start | bytes 884744 | tf_op jit(solution)/shard_map/ppermute | solution.py:265
  40.0 6.0 %weight_grad_partial.1 = (bf16[128,2304]{1,0:T(8,128)(2,1)}, bf16[128,2304]{1,0:T(8,128)(2,1)}, bf16[64,2304]{1,0:T(8,128)(2,1)}, bf16[64,2304]{1,0:T(8,128)(2,1...) custom-call(bf16[256,1024]{1,0:T(8,128)(2,1)} %get-tuple-element.33., ...), custom_call_target="tpu_custom_call" | custom-call | flops 5750000128 | bytes 8388608 | tf_op jit(solution)/shard_map/weight_grad_partial/pallas_call | solution.py:165
  46.0 8.6 %collective-permute-done.4.refs_3_.refs_4_.refs_2_ = bf16[64,2304]{1,0:T(8,128)(2,1)} collective-permute-done((bf16[64,2304]{1,0:T(8,128)(2,1)S(1)}, bf16[64,2304]{1,0:T(8,128)(2,1)}, u32[]{:S(2)}, u32[]{:S(2)}) %collective-permute-start.4) | collective-permute-done | bytes 294944 | tf_op jit(solution)/shard_map/ppermute | solution.py:261
  58.3 9.6 %all-to-all-start.1 = ((bf16[16,144,128]{2,1,0:T(8,128)(2,1)}), bf16[16,144,128]{2,1,0:T(8,128)(2,1)S(1)}, u32[]{:S(2)}, u32[]{:S(2)}) async-start(bf16[16,144,128]{2,1,0:T(8,128)(2,1)} %broadcast_in_dim.17), calls=%async_computation.1 | async-start | bytes 1179648 | tf_op jit(solution)/shard_map/all_to_all | solution.py:300
  68.9 3.0 %collective-permute-start.18 = (bf16[128,2304]{1,0:T(8,128)(2,1)}, bf16[128,2304]{1,0:T(8,128)(2,1)S(1)}, u32[]{:S(2)}, u32[]{:S(2)}) collective-permute-start(bf16[128,2304]{1,0:T(8,128)(2,1)} %get-tuple-element.54), channel_id=1, source_target_pairs={{0,6},{1,7},{2,0},{3,1},{4,2},{5,3},{6,4},{7,5},{8,14},{9,15},{10,... | collective-permute-start | bytes 1769480 | tf_op jit(solution)/shard_map/ppermute | solution.py:265
  72.0 2.7 %collective-permute-done.9.refs_9_.refs_10_.refs_8_ = bf16[64,2304]{1,0:T(8,128)(2,1)} collective-permute-done((bf16[64,2304]{1,0:T(8,128)(2,1)}, bf16[64,2304]{1,0:T(8,128)(2,1)}, u32[]{:S(2)}, u32[]{:S(2)}) %collective-permute-start.9) | collective-permute-done | bytes 294944 | tf_op jit(solution)/shard_map/ppermute | solution.py:269
  74.7 6.7 %grad_mixed.1 = (bf16[256,1024]{1,0:T(8,128)(2,1)}, bf16[256,1024]{1,0:T(8,128)(2,1)}) custom-call(bf16[256,2304]{1,0:T(8,128)(2,1)} %g0_ref.1, bf16[256,2304]{1,0:T(8,128)(2,1)} %collective-permute-done.6.refs_3_.g1_ref, bf16[128,2304]{1,0:T(8,128)(2,1)} %bitcast.30, bf16[128,2304]{1,0:T(8,128)(2,1)} %collective-permute-done.refs_2_.refs_3_.refs_1_, ...), custom_call_target="tpu_custom_call" | custom-call | flops 6899999744 | bytes 8388608 | tf_op jit(solution)/shard_map/grad_mixed/pallas_call | solution.py:207
  81.5 5.6 %branch.2 = bf16[256,2304]{1,0:T(8,128)(2,1)} custom-call(bf16[256,1024]{1,0:T(8,128)(2,1)} %collective-permute-done.3.refs_1_.refs_0_, bf16[128,2304]{1,0:T(8,128)(2,1)} %bitcast.31, bf16[128,2304]{1,0:T(8,128)(2,1)} %collective-permute-done.refs_2_.refs_3_.refs_1_, bf16[64,2304]{1,0:T(8,128)(2,1)} %collective-permute-done.4.refs_3_.refs_4_.refs_2_, ...), custom_call_target="tpu_custom_call" | custom-call | flops 5750000128 | bytes 8388608 | tf_op jit(solution)/shard_map/branch/pallas_call | solution.py:236
  87.7 7.0 %collective-permute-done.13 = bf16[128,2304]{1,0:T(8,128)(2,1)S(1)} collective-permute-done((bf16[128,2304]{1,0:T(8,128)(2,1)}, bf16[128,2304]{1,0:T(8,128)(2,1)S(1)}, u32[]{:S(2)}, u32[]{:S(2)}) %collective-permute-start.13) | collective-permute-done | bytes 589856 | tf_op jit(solution)/shard_map/ppermute | solution.py:269
  94.8 2.8 %collective-permute-start.14 = (bf16[64,2304]{1,0:T(8,128)(2,1)S(1)}, bf16[64,2304]{1,0:T(8,128)(2,1)S(1)}, u32[]{:S(2)}, u32[]{:S(2)}) collective-permute-start(bf16[64,2304]{1,0:T(8,128)(2,1)S(1)} %get-tuple-element.68), channel_id=1, source_target_pairs={{0,6},{1,7},{2,0},{3,1},{4,2},{5,3},{6,4},{7,5},{8,14},{9,15},{10,... | collective-permute-start | bytes 884744 | tf_op jit(solution)/shard_map/ppermute | solution.py:265
  100.5 10.7 %attention_backward.1 = (bf16[256,2048]{1,0:T(8,128)(2,1)}, bf16[256,1024]{1,0:T(8,128)(2,1)}, bf16[256,1024]{1,0:T(8,128)(2,1)}) custom-call(s32[9]{0:T(128)} %pad_add_fusion.place_ref, bf16[256,2048]{1,0:T(8,128)(2,1)} %q_ref.3, bf16[256,1024]{1,0:T(8,128)(2,1)} %k_ref.3, bf16[256,1024]{1,0:T(8,128)(2,1)} %v_ref.3, ...), custom_call_target="tpu_custom_call" | custom-call | flops 11500000256 | bytes 9437184 | tf_op jit(solution)/shard_map/attention_backward/pallas_call | solution.py:121
  112.2 3.2 %collective-permute-start.15 = (bf16[128,2304]{1,0:T(8,128)(2,1)}, bf16[128,2304]{1,0:T(8,128)(2,1)}, u32[]{:S(2)}, u32[]{:S(2)}) collective-permute-start(bf16[128,2304]{1,0:T(8,128)(2,1)} %add_convert_fusion.3), channel_id=1, source_target_pairs={{0,6},{1,7},{2,0},{3,1},{4,2},{5,3},{6,4},{7,5},{8,14},{9,15},{10,... | collective-permute-start | bytes 1769480 | tf_op jit(solution)/shard_map/ppermute | solution.py:265
  116.6 1.4 %copy.21 = f32[128,2304]{1,0:T(8,128)} copy(f32[128,2304]{0,1:T(8,128)S(1)} %get-tuple-element.65) | data formatting | bytes 2359296
  118.0 1.1 copy.22
  119.1 6.0 %branch.3 = bf16[256,2304]{1,0:T(8,128)(2,1)} custom-call(bf16[256,1024]{1,0:T(8,128)(2,1)} %get-tuple-element.33.refs_0_, bf16[256,2304]{1,0:T(8,128)(2,1)} %collective-permute-done.11.refs_1_, bf16[128,2304]{1,0:T(8,128)(2,1)} %bitcast.32, bf16[128,2304]{1,0:T(8,128)(2,1)} %collective-permute-done.refs_2_.refs_3_.refs_1_, ...), custom_call_target="tpu_custom_call" | custom-call | flops 5750000128 | bytes 8388608 | tf_op jit(solution)/shard_map/branch/pallas_call | solution.py:236
  125.1 1.1 collective-permute-done.15
  126.2 4.3 %collective-permute-done.17 = bf16[128,2304]{1,0:T(8,128)(2,1)} collective-permute-done((bf16[128,2304]{1,0:T(8,128)(2,1)}, bf16[128,2304]{1,0:T(8,128)(2,1)}, u32[]{:S(2)}, u32[]{:S(2)}) %collective-permute-start.17) | collective-permute-done | bytes 589856 | tf_op jit(solution)/shard_map/ppermute | solution.py:261
  130.5 2.5 %fusion.2 = bf16[1,128,2304]{2,1,0:T(8,128)(2,1)} fusion(bf16[128,2304]{1,0:T(8,128)(2,1)} %collective-permute-done.20, bf16[128,2304]{1,0:T(8,128)(2,1)} %collective-permute-done.17, bf16[128,2304]{1,0:T(8,128)(2,1)} %collective-permute-done.15, bf16[128,2304]{1,0:T(8,128)(2,1)S(1)} %copy-done.2), kind=kLoop, calls=%fused_computation.10 | loop fusion | flops 2359296 | bytes 2949120 | tf_op jit(solution)/shard_map/broadcast_in_dim | solution.py:351
  (71 shorter events, 15.4 us)
Async XLA Ops:
  0.6 30.5 %collective-permute-start = (bf16[128,2304]{1,0:T(8,128)(2,1)}, bf16[128,2304]{1,0:T(8,128)(2,1)}, u32[]{:S(2)}, u32[]{:S(2)}) collective-permute-start(bf16[128,2304]{1,0:T(8,128)(2,1)} %bitcast.27), channel_id=1, source_target_pairs={{0,6},{1,7},{2,0},{3,1},{4,2},{5,3},{6,4},{7,5},{8,14},{9,15},{10,... | collective-permute-start | bytes 1769480 | tf_op jit(solution)/shard_map/ppermute | solution.py:265
  3.5 27.7 %collective-permute-start.1 = (bf16[128,2304]{1,0:T(8,128)(2,1)}, bf16[128,2304]{1,0:T(8,128)(2,1)}, u32[]{:S(2)}, u32[]{:S(2)}) collective-permute-start(bf16[128,2304]{1,0:T(8,128)(2,1)} %bitcast.28), channel_id=1, source_target_pairs={{0,2},{1,3},{2,4},{3,5},{4,6},{5,7},{6,0},{7,1},{8,10},{9,11},{10,... | collective-permute-start | bytes 1769480 | tf_op jit(solution)/shard_map/ppermute | solution.py:261
  3.5 27.7 %collective-permute-start.2 = (bf16[128,2304]{1,0:T(8,128)(2,1)}, bf16[128,2304]{1,0:T(8,128)(2,1)}, u32[]{:S(2)}, u32[]{:S(2)}) collective-permute-start(bf16[128,2304]{1,0:T(8,128)(2,1)} %bitcast.29), channel_id=1, source_target_pairs={{0,8},{1,9},{2,10},{3,11},{4,12},{5,13},{6,14},{7,15},{8,0},{9,1},... | collective-permute-start | bytes 1769480 | tf_op jit(solution)/shard_map/ppermute | solution.py:269
  5.4 34.6 %collective-permute-start.6 = (bf16[256,2304]{1,0:T(8,128)(2,1)}, bf16[256,2304]{1,0:T(8,128)(2,1)}, u32[]{:S(2)}, u32[]{:S(2)}) collective-permute-start(bf16[256,2304]{1,0:T(8,128)(2,1)} %g0_ref.1), channel_id=1, source_target_pairs={{0,1},{1,0},{2,3},{3,2},{4,5},{5,4},{6,7},{7,6},{8,9},{9,8},{10,11... | collective-permute-start | bytes 3538952 | tf_op jit(solution)/shard_map/ppermute | solution.py:273
  7.7 48.9 %all-to-all-start = ((bf16[16,144,128]{2,1,0:T(8,128)(2,1)}), bf16[16,144,128]{2,1,0:T(8,128)(2,1)S(1)}, u32[]{:S(2)}, u32[]{:S(2)}) async-start(bf16[16,144,128]{2,1,0:T(8,128)(2,1)} %bitcast.4), calls=%async_computation | async-start | bytes 1179648 | tf_op jit(solution)/shard_map/all_to_all | solution.py:295
  29.8 6.9 %collective-permute-start.3 = (bf16[256,1024]{1,0:T(8,128)(2,1)}, bf16[256,1024]{1,0:T(8,128)(2,1)}, u32[]{:S(2)}, u32[]{:S(2)}) collective-permute-start(bf16[256,1024]{1,0:T(8,128)(2,1)} %get-tuple-element.34), channel_id=1, source_target_pairs={{0,1},{1,0},{2,3},{3,2},{4,5},{5,4},{6,7},{7,6},{8,9},{9,8},{10,11... | collective-permute-start | bytes 1572872 | tf_op jit(solution)/shard_map/ppermute | solution.py:273
  31.2 37.7 %collective-permute-start.10 = (bf16[128,2304]{1,0:T(8,128)(2,1)}, bf16[128,2304]{1,0:T(8,128)(2,1)S(1)}, u32[]{:S(2)}, u32[]{:S(2)}) collective-permute-start(bf16[128,2304]{1,0:T(8,128)(2,1)} %collective-permute-done.2.refs_6_.refs_7_.refs_5_), channel_id=1, source_target_pairs={{0,2},{1,3},{2,4},{3,5},{4,6},{5,7},{6,0},{7,1},{8,10},{9,11},{10,... | collective-permute-start | bytes 1769480 | tf_op jit(solution)/shard_map/ppermute | solution.py:261
  32.0 39.9 %collective-permute-start.7 = (bf16[128,2304]{1,0:T(8,128)(2,1)}, bf16[128,2304]{1,0:T(8,128)(2,1)}, u32[]{:S(2)}, u32[]{:S(2)}) collective-permute-start(bf16[128,2304]{1,0:T(8,128)(2,1)} %collective-permute-done.2.refs_6_.refs_7_.refs_5_), channel_id=1, source_target_pairs={{0,6},{1,7},{2,0},{3,1},{4,2},{5,3},{6,4},{7,5},{8,14},{9,15},{10,... | collective-permute-start | bytes 1769480 | tf_op jit(solution)/shard_map/ppermute | solution.py:265
  35.6 19.0 %collective-permute-start.4 = (bf16[64,2304]{1,0:T(8,128)(2,1)S(1)}, bf16[64,2304]{1,0:T(8,128)(2,1)}, u32[]{:S(2)}, u32[]{:S(2)}) collective-permute-start(bf16[64,2304]{1,0:T(8,128)(2,1)S(1)} %slice.12), channel_id=1, source_target_pairs={{0,2},{1,3},{2,4},{3,5},{4,6},{5,7},{6,0},{7,1},{8,10},{9,11},{10,... | collective-permute-start | bytes 884744 | tf_op jit(solution)/shard_map/ppermute | solution.py:261
  36.6 20.0 %copy-start.8 = (f32[128,144]{0,1:T(8,128)S(1)}, f32[128,144]{0,1:T(8,128)}, u32[]{:S(2)}) copy-start(f32[128,144]{0,1:T(8,128)} %param.16) | copy-start | bytes 221188
  36.7 17.9 %collective-permute-start.5 = (bf16[64,2304]{1,0:T(8,128)(2,1)S(1)}, bf16[64,2304]{1,0:T(8,128)(2,1)}, u32[]{:S(2)}, u32[]{:S(2)}) collective-permute-start(bf16[64,2304]{1,0:T(8,128)(2,1)S(1)} %slice.13), channel_id=1, source_target_pairs={{0,6},{1,7},{2,0},{3,1},{4,2},{5,3},{6,4},{7,5},{8,14},{9,15},{10,... | collective-permute-start | bytes 884744 | tf_op jit(solution)/shard_map/ppermute | solution.py:265
  54.6 17.4 %collective-permute-start.8 = (bf16[64,2304]{1,0:T(8,128)(2,1)}, bf16[64,2304]{1,0:T(8,128)(2,1)}, u32[]{:S(2)}, u32[]{:S(2)}) collective-permute-start(bf16[64,2304]{1,0:T(8,128)(2,1)} %collective-permute-done.4.refs_3_.refs_4_.refs_2_), channel_id=1, source_target_pairs={{0,8},{1,9},{2,10},{3,11},{4,12},{5,13},{6,14},{7,15},{8,0},{9,1},... | collective-permute-start | bytes 884744 | tf_op jit(solution)/shard_map/ppermute | solution.py:269
  55.6 19.1 %collective-permute-start.9 = (bf16[64,2304]{1,0:T(8,128)(2,1)}, bf16[64,2304]{1,0:T(8,128)(2,1)}, u32[]{:S(2)}, u32[]{:S(2)}) collective-permute-start(bf16[64,2304]{1,0:T(8,128)(2,1)} %collective-permute-done.5.refs_4_.refs_5_.refs_3_), channel_id=1, source_target_pairs={{0,8},{1,9},{2,10},{3,11},{4,12},{5,13},{6,14},{7,15},{8,0},{9,1},... | collective-permute-start | bytes 884744 | tf_op jit(solution)/shard_map/ppermute | solution.py:269
  58.3 58.0 %all-to-all-start.1 = ((bf16[16,144,128]{2,1,0:T(8,128)(2,1)}), bf16[16,144,128]{2,1,0:T(8,128)(2,1)S(1)}, u32[]{:S(2)}, u32[]{:S(2)}) async-start(bf16[16,144,128]{2,1,0:T(8,128)(2,1)} %broadcast_in_dim.17), calls=%async_computation.1 | async-start | bytes 1179648 | tf_op jit(solution)/shard_map/all_to_all | solution.py:300
  67.9 26.8 %collective-permute-start.13 = (bf16[128,2304]{1,0:T(8,128)(2,1)}, bf16[128,2304]{1,0:T(8,128)(2,1)S(1)}, u32[]{:S(2)}, u32[]{:S(2)}) collective-permute-start(bf16[128,2304]{1,0:T(8,128)(2,1)} %get-tuple-element.50), channel_id=1, source_target_pairs={{0,8},{1,9},{2,10},{3,11},{4,12},{5,13},{6,14},{7,15},{8,0},{9,1},... | collective-permute-start | bytes 1769480 | tf_op jit(solution)/shard_map/ppermute | solution.py:269
  68.9 28.7 %collective-permute-start.18 = (bf16[128,2304]{1,0:T(8,128)(2,1)}, bf16[128,2304]{1,0:T(8,128)(2,1)S(1)}, u32[]{:S(2)}, u32[]{:S(2)}) collective-permute-start(bf16[128,2304]{1,0:T(8,128)(2,1)} %get-tuple-element.54), channel_id=1, source_target_pairs={{0,6},{1,7},{2,0},{3,1},{4,2},{5,3},{6,4},{7,5},{8,14},{9,15},{10,... | collective-permute-start | bytes 1769480 | tf_op jit(solution)/shard_map/ppermute | solution.py:265
  71.9 25.7 %collective-permute-start.19 = (bf16[128,2304]{1,0:T(8,128)(2,1)S(1)}, bf16[128,2304]{1,0:T(8,128)(2,1)S(1)}, u32[]{:S(2)}, u32[]{:S(2)}) collective-permute-start(bf16[128,2304]{1,0:T(8,128)(2,1)S(1)} %copy-done.10), channel_id=1, source_target_pairs={{0,2},{1,3},{2,4},{3,5},{4,6},{5,7},{6,0},{7,1},{8,10},{9,11},{10,... | collective-permute-start | bytes 1769480 | tf_op jit(solution)/shard_map/ppermute | solution.py:261
  81.4 18.3 %collective-permute-start.12 = (bf16[256,1024]{1,0:T(8,128)(2,1)}, bf16[256,1024]{1,0:T(8,128)(2,1)S(1)}, u32[]{:S(2)}, u32[]{:S(2)}) collective-permute-start(bf16[256,1024]{1,0:T(8,128)(2,1)} %get-tuple-element.43), channel_id=1, source_target_pairs={{0,1},{1,0},{2,3},{3,2},{4,5},{5,4},{6,7},{7,6},{8,9},{9,8},{10,11... | collective-permute-start | bytes 1572872 | tf_op jit(solution)/shard_map/ppermute | solution.py:273
  87.1 32.0 %collective-permute-start.11 = (bf16[256,2304]{1,0:T(8,128)(2,1)}, bf16[256,2304]{1,0:T(8,128)(2,1)}, u32[]{:S(2)}, u32[]{:S(2)}) collective-permute-start(bf16[256,2304]{1,0:T(8,128)(2,1)} %branch.2), channel_id=1, source_target_pairs={{0,1},{1,0},{2,3},{3,2},{4,5},{5,4},{6,7},{7,6},{8,9},{9,8},{10,11... | collective-permute-start | bytes 3538952 | tf_op jit(solution)/shard_map/ppermute | solution.py:273
  94.8 16.4 %collective-permute-start.14 = (bf16[64,2304]{1,0:T(8,128)(2,1)S(1)}, bf16[64,2304]{1,0:T(8,128)(2,1)S(1)}, u32[]{:S(2)}, u32[]{:S(2)}) collective-permute-start(bf16[64,2304]{1,0:T(8,128)(2,1)S(1)} %get-tuple-element.68), channel_id=1, source_target_pairs={{0,6},{1,7},{2,0},{3,1},{4,2},{5,3},{6,4},{7,5},{8,14},{9,15},{10,... | collective-permute-start | bytes 884744 | tf_op jit(solution)/shard_map/ppermute | solution.py:265
  97.6 17.8 %collective-permute-start.16 = (bf16[64,2304]{1,0:T(8,128)(2,1)S(1)}, bf16[64,2304]{1,0:T(8,128)(2,1)S(1)}, u32[]{:S(2)}, u32[]{:S(2)}) collective-permute-start(bf16[64,2304]{1,0:T(8,128)(2,1)S(1)} %get-tuple-element.69), channel_id=1, source_target_pairs={{0,2},{1,3},{2,4},{3,5},{4,6},{5,7},{6,0},{7,1},{8,10},{9,11},{10,... | collective-permute-start | bytes 884744 | tf_op jit(solution)/shard_map/ppermute | solution.py:261
  98.7 26.4 %collective-permute-start.20 = (bf16[128,2304]{1,0:T(8,128)(2,1)}, bf16[128,2304]{1,0:T(8,128)(2,1)}, u32[]{:S(2)}, u32[]{:S(2)}) collective-permute-start(bf16[128,2304]{1,0:T(8,128)(2,1)} %add_convert_fusion.1), channel_id=1, source_target_pairs={{0,8},{1,9},{2,10},{3,11},{4,12},{5,13},{6,14},{7,15},{8,0},{9,1},... | collective-permute-start | bytes 1769480 | tf_op jit(solution)/shard_map/ppermute | solution.py:269
  112.2 14.0 %collective-permute-start.15 = (bf16[128,2304]{1,0:T(8,128)(2,1)}, bf16[128,2304]{1,0:T(8,128)(2,1)}, u32[]{:S(2)}, u32[]{:S(2)}) collective-permute-start(bf16[128,2304]{1,0:T(8,128)(2,1)} %add_convert_fusion.3), channel_id=1, source_target_pairs={{0,6},{1,7},{2,0},{3,1},{4,2},{5,3},{6,4},{7,5},{8,14},{9,15},{10,... | collective-permute-start | bytes 1769480 | tf_op jit(solution)/shard_map/ppermute | solution.py:265
  116.3 14.2 %collective-permute-start.17 = (bf16[128,2304]{1,0:T(8,128)(2,1)}, bf16[128,2304]{1,0:T(8,128)(2,1)}, u32[]{:S(2)}, u32[]{:S(2)}) collective-permute-start(bf16[128,2304]{1,0:T(8,128)(2,1)} %add_convert_fusion.2), channel_id=1, source_target_pairs={{0,2},{1,3},{2,4},{3,5},{4,6},{5,7},{6,0},{7,1},{8,10},{9,11},{10,... | collective-permute-start | bytes 1769480 | tf_op jit(solution)/shard_map/ppermute | solution.py:261
  (11 other events, 96.5 us)

commit v3 on v2

v3 whole, which is shorter than its diff:
```python
import math

import jax
import jax.numpy as jnp
from jax import lax
from jax.experimental import pallas as pl
from jax.experimental.pallas import tpu as pltpu
from jax.sharding import PartitionSpec as P

HEADS = 16
KV_HEADS = 8
HEAD_DIM = 128

query_scale = 1.0 / 12.0
outer_rate = 0.7
outer_moment = 0.9
mix_factor = 0.5

X_SIZE = 4
Z_SIZE = 2
VMEM_LIMIT = 56 * 1024 * 1024

NT = (((1,), (1,)), ((), ()))
TN = (((0,), (0,)), ((), ()))


def f32_dot(left, right, dims=(((1,), (0,)), ((), ()))):
    return lax.dot_general(left, right, dims, preferred_element_type=jnp.float32)


def params(**kwargs):
    return pltpu.CompilerParams(vmem_limit_bytes=VMEM_LIMIT, **kwargs)


def cost(microseconds, bytes_accessed):
    return pl.CostEstimate(
        flops=int(microseconds * 2.300e+07), bytes_accessed=bytes_accessed, transcendentals=0
    )


SLOT_Z = (0, 0, 0, 1, 1, 0, 1, 1)
SLOT_X = (0, 1, 3, 0, 1, 2, 3, 2)

ROW_BLOCKS = ((0, 128, 128), (128, 64, 256), (192, 64, 256))


def own_lanes(place_ref, turn):
    parity = place_ref[KV_HEADS] if turn == 0 else 1 - place_ref[KV_HEADS]
    return pl.ds(pl.multiple_of(parity * HEAD_DIM, HEAD_DIM), HEAD_DIM)


def both_heads(place_ref, ref):
    return jnp.concatenate([ref[:, own_lanes(place_ref, turn)] for turn in range(2)], axis=0)


def attention_of(scores):
    def block(turn, first, rows, seen):
        part = scores[pl.ds(turn * scores.shape[1] + first, rows), :seen]
        allowed = first + lax.broadcasted_iota(
            jnp.int32, (rows, seen), 0
        ) >= lax.broadcasted_iota(jnp.int32, (rows, seen), 1)
        part = jnp.where(allowed, part, -jnp.inf)
        highest = jnp.max(part, axis=-1, keepdims=True)
        terms = jnp.exp2((part - highest) * (query_scale * math.log2(math.e)))
        return terms * (1.0 / jnp.sum(terms, axis=-1, keepdims=True))

    return block


def put_rounded(ref, turn, first, rows, seen, values):
    length = ref.shape[1]
    stacked = pl.ds(turn * length + first, rows)
    ref[stacked, :seen] = values.astype(jnp.bfloat16)
    if seen < length:
        ref[stacked, seen:] = jnp.zeros((rows, length - seen), jnp.bfloat16)


def forward_kernel(place_ref, q_ref, k_ref, v_ref, own_ref, other_ref, scores_ref, rounded_ref):
    length = q_ref.shape[0]
    scores_ref[...] = f32_dot(both_heads(place_ref, q_ref), k_ref[...], NT)
    attention = attention_of(scores_ref)
    for turn in range(2):
        for block in ROW_BLOCKS:
            put_rounded(rounded_ref, turn, *block, attention(turn, *block))
    mixed = f32_dot(rounded_ref[...], v_ref[...]).astype(jnp.bfloat16)
    own_ref[...] = mixed[:length]
    other_ref[...] = mixed[length:]


def slot_specs(length):
    return (
        pl.BlockSpec((length, 2 * HEAD_DIM), lambda r, place: (0, place[r])),
        pl.BlockSpec((length, HEAD_DIM), lambda r, place: (0, place[r])),
        pl.BlockSpec((length, HEAD_DIM), lambda r, place: (0, r)),
    )


def forward(place, query_states, key_states, value_states):
    length = query_states.shape[0]
    pair_spec, kv_spec, slot_spec = slot_specs(length)
    out = jax.ShapeDtypeStruct((length, KV_HEADS * HEAD_DIM), jnp.bfloat16)
    return pl.pallas_call(
        forward_kernel,
        grid_spec=pltpu.PrefetchScalarGridSpec(
            num_scalar_prefetch=1,
            grid=(KV_HEADS,),
            in_specs=[pair_spec, kv_spec, kv_spec],
            out_specs=[slot_spec, slot_spec],
            scratch_shapes=[
                pltpu.VMEM((2 * length, length), jnp.float32),
                pltpu.VMEM((2 * length, length), jnp.bfloat16),
            ],
        ),
        out_shape=[out, out],
        compiler_params=params(),
        cost_estimate=cost(7, 4 * 2**20),
        name="attention_forward",
    )(place, query_states, key_states, value_states)


def backward_kernel(place_ref, q_ref, k_ref, v_ref, own_ref, other_ref, *refs):
    dq_ref, dk_ref, dv_ref, scores_ref, probs_ref, grad_scores_ref, rounded_ref = refs
    length = q_ref.shape[0]
    queries = both_heads(place_ref, q_ref)
    grad_mixed = jnp.concatenate([own_ref[...], other_ref[...]], axis=0)
    scores_ref[...] = f32_dot(queries, k_ref[...], NT)
    probs_ref[...] = f32_dot(grad_mixed, v_ref[...], NT)
    attention_block = attention_of(scores_ref)
    for turn in range(2):
        for block in ROW_BLOCKS:
            first, rows, seen = block
            attention = attention_block(turn, *block)
            grad_probs = probs_ref[pl.ds(turn * length + first, rows), :seen]
            row_term = jnp.sum(attention * grad_probs, axis=-1, keepdims=True)
            grad_scores = attention * (grad_probs - row_term) * query_scale
            put_rounded(grad_scores_ref, turn, *block, grad_scores)
            put_rounded(rounded_ref, turn, *block, attention)
    dv_ref[...] = f32_dot(rounded_ref[...], grad_mixed, TN).astype(jnp.bfloat16)
    dk_ref[...] = f32_dot(grad_scores_ref[...], queries, TN).astype(jnp.bfloat16)
    dq = f32_dot(grad_scores_ref[...], k_ref[...]).astype(jnp.bfloat16)
    for turn in range(2):
        dq_ref[:, own_lanes(place_ref, turn)] = dq[turn * length : (turn + 1) * length]


def backward(place, query_states, key_states, value_states, grad_own, grad_other):
    length = query_states.shape[0]
    pair_spec, kv_spec, slot_spec = slot_specs(length)
    return pl.pallas_call(
        backward_kernel,
        grid_spec=pltpu.PrefetchScalarGridSpec(
            num_scalar_prefetch=1,
            grid=(KV_HEADS,),
            in_specs=[pair_spec, kv_spec, kv_spec, slot_spec, slot_spec],
            out_specs=[pair_spec, kv_spec, kv_spec],
            scratch_shapes=[
                pltpu.VMEM((2 * length, length), jnp.float32),
                pltpu.VMEM((2 * length, length), jnp.float32),
                pltpu.VMEM((2 * length, length), jnp.bfloat16),
                pltpu.VMEM((2 * length, length), jnp.bfloat16),
            ],
        ),
        out_shape=[
            jax.ShapeDtypeStruct(query_states.shape, jnp.bfloat16),
            jax.ShapeDtypeStruct(key_states.shape, jnp.bfloat16),
            jax.ShapeDtypeStruct(value_states.shape, jnp.bfloat16),
        ],
        compiler_params=params(),
        cost_estimate=cost(10, 9 * 2**20),
        name="attention_backward",
    )(place, query_states, key_states, value_states, grad_own, grad_other)


COLUMN_TILES = 3


def weight_grad_kernel(m0_ref, m1_ref, g0_ref, g1_ref, *refs):
    *out_refs, mixed_ref = refs
    length = m0_ref.shape[0]

    @pl.when(pl.program_id(0) == 0)
    def _():
        mixed_ref[:, :length] = m0_ref[...].T
        mixed_ref[:, length:] = m1_ref[...].T

    grads = jnp.concatenate([g0_ref[...], g1_ref[...]], axis=0)
    product = f32_dot(mixed_ref[...], grads).astype(jnp.bfloat16)
    for slot, out_ref in enumerate(out_refs):
        out_ref[...] = product[slot * HEAD_DIM : (slot + 1) * HEAD_DIM]


def weight_grad_pieces(mixed_own, mixed_peer, grad_own, grad_peer):
    length, half = mixed_own.shape
    width = grad_own.shape[1]
    tile = width // COLUMN_TILES
    whole = pl.BlockSpec((length, half), lambda j: (0, 0))
    part = pl.BlockSpec((length, tile), lambda j: (0, j))
    return pl.pallas_call(
        weight_grad_kernel,
        grid=(COLUMN_TILES,),
        in_specs=[whole, whole, part, part],
        out_specs=[pl.BlockSpec((HEAD_DIM, tile), lambda j: (0, j))] * KV_HEADS,
        out_shape=[jax.ShapeDtypeStruct((HEAD_DIM, width), jnp.bfloat16)] * KV_HEADS,
        scratch_shapes=[pltpu.VMEM((half, 2 * length), jnp.bfloat16)],
        compiler_params=params(),
        cost_estimate=cost(5, 8 * 2**20),
        name="weight_grad_partial",
    )(mixed_own, mixed_peer, grad_own, grad_peer)


def project_kernel(g0_ref, g1_ref, m0_ref, m1_ref, *refs):
    *pieces, grad0_ref, grad1_ref, branch0_ref, branch1_ref, sum_ref = refs
    step = pl.program_id(0)
    length = g0_ref.shape[0]
    weight = jnp.concatenate([piece[...] for piece in pieces], axis=0)
    part = f32_dot(jnp.concatenate([g0_ref[...], g1_ref[...]], axis=0), weight, NT)

    @pl.when(step == 0)
    def _():
        sum_ref[...] = part

    @pl.when((step > 0) & (step < COLUMN_TILES - 1))
    def _():
        sum_ref[...] += part

    @pl.when(step == COLUMN_TILES - 1)
    def _():
        total = (sum_ref[...] + part).astype(jnp.bfloat16)
        grad0_ref[...] = total[:length]
        grad1_ref[...] = total[length:]

    branch = f32_dot(jnp.concatenate([m0_ref[...], m1_ref[...]], axis=0), weight)
    branch = branch.astype(jnp.bfloat16)
    branch0_ref[...] = branch[:length]
    branch1_ref[...] = branch[length:]


def project(grad_own, grad_peer, mixed_own, mixed_peer, pieces):
    length, width = grad_own.shape
    half = mixed_own.shape[1]
    tile = width // COLUMN_TILES
    part = pl.BlockSpec((length, tile), lambda j: (0, j))
    whole = pl.BlockSpec((length, half), lambda j: (0, 0))
    return pl.pallas_call(
        project_kernel,
        grid=(COLUMN_TILES,),
        in_specs=[part, part, whole, whole]
        + [pl.BlockSpec((HEAD_DIM, tile), lambda j: (0, j))] * len(pieces),
        out_specs=[whole, whole, part, part],
        out_shape=[jax.ShapeDtypeStruct((length, half), jnp.bfloat16)] * 2
        + [jax.ShapeDtypeStruct((length, width), jnp.bfloat16)] * 2,
        scratch_shapes=[pltpu.VMEM((2 * length, half), jnp.float32)],
        compiler_params=params(),
        cost_estimate=cost(11, 14 * 2**20),
        name="project",
    )(grad_own, grad_peer, mixed_own, mixed_peer, *pieces)


def update_kernel(steps_ref, anchor_ref, local_ref, anchor_out_ref, merged_ref):
    for start in range(0, anchor_ref.shape[1], HEAD_DIM):
        columns = pl.ds(start, HEAD_DIM)
        step = steps_ref[columns, :].astype(jnp.float32).T
        anchor_new = anchor_ref[:, columns] - outer_rate * step
        anchor_out_ref[:, columns] = anchor_new
        merged = mix_factor * local_ref[:, columns].astype(jnp.float32) + mix_factor * anchor_new
        merged_ref[:, columns] = merged.astype(jnp.bfloat16)


def shift(dz, dx, dcore):
    pairs = []
    for z in range(Z_SIZE):
        for x in range(X_SIZE):
            for core in range(2):
                target = ((z + dz) % Z_SIZE) * X_SIZE + (x + dx) % X_SIZE
                pairs.append(((z * X_SIZE + x) * 2 + core, target * 2 + (core + dcore) % 2))
    return pairs


def to_right(array):
    return lax.ppermute(array, "fsdp", shift(0, 1, 0))


def to_left(array):
    return lax.ppermute(array, "fsdp", shift(0, -1, 0))


def to_far(array):
    return lax.ppermute(array, "fsdp", shift(1, 0, 0))


def to_peer(array):
    return lax.ppermute(array, "fsdp", shift(0, 0, 1))


def added(*terms):
    total = terms[0].astype(jnp.float32)
    for term in terms[1:]:
        total = total + term.astype(jnp.float32)
    return total.astype(jnp.bfloat16)


def place_table():
    position = lax.axis_index("fsdp")
    z, x, core = position // (2 * X_SIZE), (position // 2) % X_SIZE, position % 2
    slot_z, slot_x = jnp.array(SLOT_Z, jnp.int32), jnp.array(SLOT_X, jnp.int32)
    heads = ((z + slot_z) % Z_SIZE) * X_SIZE + (x + slot_x) % X_SIZE
    return jnp.concatenate([heads, core[None]]).astype(jnp.int32)


def packed_shares(own_delta):
    rows, replicas = own_delta.shape[0], lax.axis_size("rep")
    shares = own_delta.astype(jnp.bfloat16).reshape(rows, replicas, -1)
    return shares.transpose(1, 2, 0)


def outer_share(packed, momentum):
    replicas = lax.axis_size("rep")
    shares = lax.all_to_all(packed, "rep", 0, 0, tiled=False)
    mean_share = jnp.sum(shares.astype(jnp.float32), axis=0).T / replicas
    momentum_new = outer_moment * momentum + mean_share
    step_share = (outer_moment * momentum_new + mean_share).astype(jnp.bfloat16).T
    return momentum_new, jnp.broadcast_to(step_share[None], (replicas, *step_share.shape))


def outer_update(steps, anchor, local):
    rows, width = anchor.shape
    tile = width // COLUMN_TILES
    steps = lax.all_to_all(steps, "rep", 0, 0, tiled=False).reshape(width, rows)
    part = pl.BlockSpec((rows, tile), lambda j: (0, j))
    return pl.pallas_call(
        update_kernel,
        grid=(COLUMN_TILES,),
        in_specs=[pl.BlockSpec((tile, rows), lambda j: (j, 0)), part, part],
        out_specs=[part, part],
        out_shape=[
            jax.ShapeDtypeStruct(anchor.shape, jnp.float32),
            jax.ShapeDtypeStruct(local.shape, jnp.bfloat16),
        ],
        compiler_params=params(),
        cost_estimate=cost(3, 4 * 2**20),
        name="outer_update",
    )(steps, anchor, local)


def on_device(
    query_states,
    key_states,
    value_states,
    output_grad,
    out_weight,
    pseudo_grad,
    anchor,
    momentum,
    local_weight,
):
    place = place_table()
    own_rows = out_weight[0]
    grad_peer = to_peer(output_grad)

    w3 = to_right(own_rows)
    w1 = to_left(own_rows)
    w4 = to_far(own_rows)
    mixed_own, mixed_other = forward(place, query_states, key_states, value_states)
    mixed_peer = to_peer(mixed_other)
    w1, w3, w4, mixed_own = lax.optimization_barrier((w1, w3, w4, mixed_own))
    w2 = to_right(w3)
    w5 = to_left(w4)
    w7 = to_right(w4)

    d0, d1, d3, d4, d5, d2, d7, d6 = weight_grad_pieces(
        mixed_own, mixed_peer, output_grad, grad_peer
    )
    w5, w2, d6 = lax.optimization_barrier((w5, w2, d6))
    w6 = to_left(w5)
    r2 = to_far(d6)
    r1f = to_far(d5)
    w6, d7 = lax.optimization_barrier((w6, d7))
    r4 = to_left(d7)
    d0, pseudo_grad = lax.optimization_barrier((d0, pseudo_grad))
    momentum_new, steps = outer_share(packed_shares(pseudo_grad[0]), momentum)
    w7, d2 = lax.optimization_barrier((w7, d2))
    s2 = added(d2, r2)
    w6, w7, s2 = lax.optimization_barrier((w6, w7, s2))
    r1 = to_right(s2)
    grad_mixed, grad_send, branch_own, branch_send = project(
        output_grad, grad_peer, mixed_own, mixed_peer, [own_rows, w1, w3, w4, w5, w2, w7, w6]
    )
    s1 = added(d1, r1f, r1)
    s4 = added(d4, r4)
    grad_mixed, s1, s4, steps = lax.optimization_barrier((grad_mixed, s1, s4, steps))
    d3, s4 = lax.optimization_barrier((d3, s4))
    from_right = to_left(d3)
    from_left = to_right(s1)
    from_far = to_far(s4)
    weight_grad = added(d0, from_right, from_left, from_far)[None]
    grad_query, grad_key, grad_value = backward(
        place, query_states, key_states, value_states, grad_mixed, to_peer(grad_send)
    )
    branch_out = added(branch_own, to_peer(branch_send))

    anchor_new, merged = outer_update(steps, anchor, local_weight[0])
    return (
        branch_out,
        grad_query,
        grad_key,
        grad_value,
        weight_grad,
        anchor_new,
        momentum_new,
        merged[None],
    )


def solution(mesh):
    return jax.shard_map(
        on_device,
        mesh=mesh,
        in_specs=(
            P(("rep", "fsdp"), None),
            P(("rep", "fsdp"), None),
            P(("rep", "fsdp"), None),
            P(("rep", "fsdp"), None),
            P("rep", "fsdp", None),
            P("rep", "fsdp", None),
            P("fsdp", None),
            P("fsdp", "rep"),
            P("rep", "fsdp", None),
        ),
        out_specs=(
            P(("rep", "fsdp"), None),
            P(("rep", "fsdp"), None),
            P(("rep", "fsdp"), None),
            P(("rep", "fsdp"), None),
            P("rep", "fsdp", None),
            P("fsdp", None),
            P("fsdp", "rep"),
            P("rep", "fsdp", None),
        ),
        check_vma=False,
    )
```

time: 134 us -> 118 us (0.88)
  starting transfers between devices: 45.6 us -> 36.5 us
  local copies, waits for them, and re-layouts: 9.83 us -> 4.66 us
  Pallas kernels: 45.8 us -> 40.8 us
  waiting for transfers between devices: 23.8 us -> 25.9 us
    ppermute x6 -> x5, starting transfers between devices: 17.8 us -> 5.28 us  [to_left(): return lax.ppermute(array, 'fsdp', shift(0, -1, 0))]
    all_to_all x2, waiting for transfers between devices: 0.01 us -> 8.62 us  [the longest x1 5.96 us: outer_share(): shares = lax.all_to_all(packed, 'rep', 0, 0, tiled=False)]
    ppermute x5 -> x4, waiting for transfers between devices: 9.77 us -> 2.98 us  [to_far(): return lax.ppermute(array, 'fsdp', shift(1, 0, 0))]
    ppermute x6 -> x5, waiting for transfers between devices: 12.9 us -> 7.97 us  [to_right(): return lax.ppermute(array, 'fsdp', shift(0, 1, 0))]
    unnamed x29 -> x26, local copies, waits for them, and re-layouts: 6.95 us -> 2.65 us
    ppermute x6 -> x5, waiting for transfers between devices: 1.07 us -> 4.26 us  [to_left(): return lax.ppermute(array, 'fsdp', shift(0, -1, 0))]
    pallas_call x4 -> x3, Pallas kernels: 24.3 us -> 21.4 us  [the longest x1 11.3 us: project(): pl.pallas_call(project_kernel, grid=(COLUMN_TILES,), in_specs=[part, part...]
    ppermute x6 -> x5, starting transfers between devices: 0.93 us -> 3.14 us  [to_right(): return lax.ppermute(array, 'fsdp', shift(0, 1, 0))]
  transfers between devices with their start and end apart: 23 -> 20, of which waited for: 5 -> 9; matrix products, arithmetic and copies ran while one was open for 10% -> 6% of each run, Pallas kernels for 34% -> 32%
where the time goes in v3:
time: 118 us; the launch traced here: 116 us
  Pallas kernels  40.8 us (35%)
  starting transfers between devices  36.5 us (31%)
  waiting for transfers between devices  25.9 us (22%)
  other arithmetic  7.35 us (6%)
  local copies, waits for them, and re-layouts  4.66 us (4%)
    pallas_call x1, Pallas kernels, project(): pl.pallas_call(project_kernel, grid=(COLUMN_TILES,), in_specs=[part, part...  11.3 us
    pallas_call x1, Pallas kernels, backward(): pl.pallas_call(backward_kernel, grid_spec=pltpu.PrefetchScalarGridSpec(nu...  10.8 us
    all_to_all x1, starting transfers between devices, outer_share(): shares = lax.all_to_all(packed, 'rep', 0, 0, tiled=False)  10.7 us
    all_to_all x1, starting transfers between devices, outer_update(): steps = lax.all_to_all(steps, 'rep', 0, 0, tiled=False).reshape(width, rows)  10.6 us
    pallas_call x1, Pallas kernels, forward(): pl.pallas_call(forward_kernel, grid_spec=pltpu.PrefetchScalarGridSpec(num...  8.63 us
    ppermute x5, waiting for transfers between devices, to_right(): return lax.ppermute(array, 'fsdp', shift(0, 1, 0))  7.97 us
    pallas_call x1, Pallas kernels, weight_grad_pieces(): pl.pallas_call(weight_grad_kernel, grid=(COLUMN_TILES,), in_specs=[whole,...  6.19 us
    ppermute x4, starting transfers between devices, to_far(): return lax.ppermute(array, 'fsdp', shift(1, 0, 0))  6.09 us
  transfers between devices with their start and end apart: 20, of which 9 were waited for; matrix products, arithmetic and copies ran while one was open for 6% of the time, Pallas kernels for 32%

profile of v3, /device:TPU:8, one launch (start us, length us, event | category | flops | bytes accessed | tf_op | source)
XLA Modules:
  0.0 115.9 jit_solution(18050885415243749826)
XLA Ops:
  0.7 2.8 %collective-permute-start.1 = (bf16[128,2304]{1,0:T(8,128)(2,1)}, bf16[128,2304]{1,0:T(8,128)(2,1)S(1)}, u32[]{:S(2)}, u32[]{:S(2)}) collective-permute-start(bf16[128,2304]{1,0:T(8,128)(2,1)} %bitcast.22), channel_id=1, source_target_pairs={{0,6},{1,7},{2,0},{3,1},{4,2},{5,3},{6,4},{7,5},{8,14},{9,15},{10,... | collective-permute-start | bytes 1769480 | tf_op jit(solution)/shard_map/ppermute | solution.py:283
  3.6 1.9 %collective-permute-start.3 = (bf16[128,2304]{1,0:T(8,128)(2,1)}, bf16[128,2304]{1,0:T(8,128)(2,1)}, u32[]{:S(2)}, u32[]{:S(2)}) collective-permute-start(bf16[128,2304]{1,0:T(8,128)(2,1)} %bitcast.24), channel_id=1, source_target_pairs={{0,8},{1,9},{2,10},{3,11},{4,12},{5,13},{6,14},{7,15},{8,0},{9,1},... | collective-permute-start | bytes 1769480 | tf_op jit(solution)/shard_map/ppermute | solution.py:287
  6.8 8.6 %attention_forward.1 = (bf16[256,1024]{1,0:T(8,128)(2,1)}, bf16[256,1024]{1,0:T(8,128)(2,1)}) custom-call(s32[9]{0:T(128)} %pad_add_fusion.place_ref, bf16[256,2048]{1,0:T(8,128)(2,1)} %q_ref.3, bf16[256,1024]{1,0:T(8,128)(2,1)} %k_ref.3, bf16[256,1024]{1,0:T(8,128)(2,1)} %v_ref.3), custom_call_target="tpu_custom_call" | custom-call | flops 161000000 | bytes 4194304 | tf_op jit(solution)/shard_map/attention_forward/pallas_call | solution.py:102
  15.4 1.6 %collective-permute-done.1.refs_1_ = bf16[128,2304]{1,0:T(8,128)(2,1)S(1)} collective-permute-done((bf16[128,2304]{1,0:T(8,128)(2,1)}, bf16[128,2304]{1,0:T(8,128)(2,1)S(1)}, u32[]{:S(2)}, u32[]{:S(2)}) %collective-permute-start.1) | collective-permute-done | bytes 589856 | tf_op jit(solution)/shard_map/ppermute | solution.py:283
  17.1 3.3 %collective-permute-done.2.refs_2_ = bf16[128,2304]{1,0:T(8,128)(2,1)S(1)} collective-permute-done((bf16[128,2304]{1,0:T(8,128)(2,1)}, bf16[128,2304]{1,0:T(8,128)(2,1)S(1)}, u32[]{:S(2)}, u32[]{:S(2)}) %collective-permute-start.2) | collective-permute-done | bytes 589856 | tf_op jit(solution)/shard_map/ppermute | solution.py:279
  20.4 2.1 %collective-permute-start.5 = (bf16[128,2304]{1,0:T(8,128)(2,1)}, bf16[128,2304]{1,0:T(8,128)(2,1)}, u32[]{:S(2)}, u32[]{:S(2)}) collective-permute-start(bf16[128,2304]{1,0:T(8,128)(2,1)} %collective-permute-done.3.refs_3_), channel_id=1, source_target_pairs={{0,6},{1,7},{2,0},{3,1},{4,2},{5,3},{6,4},{7,5},{8,14},{9,15},{10,... | collective-permute-start | bytes 1769480 | tf_op jit(solution)/shard_map/ppermute | solution.py:283
  22.6 2.0 %collective-permute-done.4.m1_ref = bf16[256,1024]{1,0:T(8,128)(2,1)S(1)} collective-permute-done((bf16[256,1024]{1,0:T(8,128)(2,1)}, bf16[256,1024]{1,0:T(8,128)(2,1)S(1)}, u32[]{:S(2)}, u32[]{:S(2)}) %collective-permute-start.4) | collective-permute-done | bytes 524320 | tf_op jit(solution)/shard_map/ppermute | solution.py:291
  26.5 6.2 %weight_grad_partial.1 = (bf16[128,2304]{1,0:T(8,128)(2,1)}, bf16[128,2304]{1,0:T(8,128)(2,1)}, bf16[128,2304]{1,0:T(8,128)(2,1)}, bf16[128,2304]{1,0:T(8,128)(2...) custom-call(bf16[256,1024]{1,0:T(8,128)(2,1)} %get-tuple-element.50., ...), custom_call_target="tpu_custom_call" | custom-call | flops 115000000 | bytes 8388608 | tf_op jit(solution)/shard_map/weight_grad_partial/pallas_call | solution.py:197
  32.6 2.6 %collective-permute-done.5.refs_4_ = bf16[128,2304]{1,0:T(8,128)(2,1)} collective-permute-done((bf16[128,2304]{1,0:T(8,128)(2,1)}, bf16[128,2304]{1,0:T(8,128)(2,1)}, u32[]{:S(2)}, u32[]{:S(2)}) %collective-permute-start.5) | collective-permute-done | bytes 589856 | tf_op jit(solution)/shard_map/ppermute | solution.py:283
  35.3 4.7 %collective-permute-done.6.refs_5_ = bf16[128,2304]{1,0:T(8,128)(2,1)S(1)} collective-permute-done((bf16[128,2304]{1,0:T(8,128)(2,1)S(1)}, bf16[128,2304]{1,0:T(8,128)(2,1)S(1)}, u32[]{:S(2)}, u32[]{:S(2)}) %collective-permute-start.6) | collective-permute-done | bytes 589856 | tf_op jit(solution)/shard_map/ppermute | solution.py:279
  39.9 1.8 %collective-permute-start.9 = (bf16[128,2304]{1,0:T(8,128)(2,1)}, bf16[128,2304]{1,0:T(8,128)(2,1)S(1)}, u32[]{:S(2)}, u32[]{:S(2)}) collective-permute-start(bf16[128,2304]{1,0:T(8,128)(2,1)} %get-tuple-element.63), channel_id=1, source_target_pairs={{0,8},{1,9},{2,10},{3,11},{4,12},{5,13},{6,14},{7,15},{8,0},{9,1},... | collective-permute-start | bytes 1769480 | tf_op jit(solution)/shard_map/ppermute | solution.py:287
  42.9 10.7 %all-to-all-start = ((bf16[16,144,128]{2,1,0:T(8,128)(2,1)}), bf16[16,144,128]{2,1,0:T(8,128)(2,1)S(1)}, u32[]{:S(2)}, u32[]{:S(2)}) async-start(bf16[16,144,128]{2,1,0:T(8,128)(2,1)} %bitcast.3), calls=%async_computation | async-start | bytes 1179648 | tf_op jit(solution)/shard_map/all_to_all | solution.py:317
  55.7 1.4 %collective-permute-start.12 = (bf16[128,2304]{1,0:T(8,128)(2,1)S(1)}, bf16[128,2304]{1,0:T(8,128)(2,1)S(1)}, u32[]{:S(2)}, u32[]{:S(2)}) collective-permute-start(bf16[128,2304]{1,0:T(8,128)(2,1)S(1)} %add_convert_fusion.4), channel_id=1, source_target_pairs={{0,2},{1,3},{2,4},{3,5},{4,6},{5,7},{6,0},{7,1},{8,10},{9,11},{10,... | collective-permute-start | bytes 1769480 | tf_op jit(solution)/shard_map/ppermute | solution.py:279
  57.1 11.3 %project.1 = (bf16[256,1024]{1,0:T(8,128)(2,1)}, bf16[256,1024]{1,0:T(8,128)(2,1)}, bf16[256,2304]{1,0:T(8,128)(2,1)}, bf16[256,2304]{1,0:T(8,128)(2,1)}) custom-call(bf16[256,2304]{1,0:T(8,128)(2,1)} %g0_ref.3, bf16[256,2304]{1,0:T(8,128)(2,1)} %copy-done, bf16[256,1024]{1,0:T(8,128)(2,1)} %get-tuple-element.50.m0_ref, bf16[256,1024]{1,0:T(8,128)(2,1)} %copy-done.2, ...), custom_call_target="tpu_custom_call" | custom-call | flops 253000000 | bytes 14680064 | tf_op jit(solution)/shard_map/project/pallas_call | solution.py:243
  68.4 6.0 %all-to-all-done = bf16[16,144,128]{2,1,0:T(8,128)(2,1)S(1)} async-done(((bf16[16,144,128]{2,1,0:T(8,128)(2,1)}), bf16[16,144,128]{2,1,0:T(8,128)(2,1)S(1)}, u32[]{:S(2)}, u32[]{:S(2)}) %all-to-all-start) | async-done | bytes 589856 | tf_op jit(solution)/shard_map/all_to_all | solution.py:317
  75.3 2.1 %collective-permute-done.11 = bf16[128,2304]{1,0:T(8,128)(2,1)} collective-permute-done((bf16[128,2304]{1,0:T(8,128)(2,1)}, bf16[128,2304]{1,0:T(8,128)(2,1)}, u32[]{:S(2)}, u32[]{:S(2)}) %collective-permute-start.11) | collective-permute-done | bytes 589856 | tf_op jit(solution)/shard_map/ppermute | solution.py:287
  79.9 1.3 %collective-permute-start.17 = (bf16[128,2304]{1,0:T(8,128)(2,1)S(1)}, bf16[128,2304]{1,0:T(8,128)(2,1)}, u32[]{:S(2)}, u32[]{:S(2)}) collective-permute-start(bf16[128,2304]{1,0:T(8,128)(2,1)S(1)} %add_convert_fusion.2), channel_id=1, source_target_pairs={{0,8},{1,9},{2,10},{3,11},{4,12},{5,13},{6,14},{7,15},{8,0},{9,1},... | collective-permute-start | bytes 1769480 | tf_op jit(solution)/shard_map/ppermute | solution.py:287
  81.2 1.6 %collective-permute-start.16 = (bf16[128,2304]{1,0:T(8,128)(2,1)S(1)}, bf16[128,2304]{1,0:T(8,128)(2,1)}, u32[]{:S(2)}, u32[]{:S(2)}) collective-permute-start(bf16[128,2304]{1,0:T(8,128)(2,1)S(1)} %add_convert_fusion.3), channel_id=1, source_target_pairs={{0,2},{1,3},{2,4},{3,5},{4,6},{5,7},{6,0},{7,1},{8,10},{9,11},{10,... | collective-permute-start | bytes 1769480 | tf_op jit(solution)/shard_map/ppermute | solution.py:279
  83.4 10.6 %all-to-all-start.1 = ((bf16[16,144,128]{2,1,0:T(8,128)(2,1)}), bf16[16,144,128]{2,1,0:T(8,128)(2,1)S(1)}, u32[]{:S(2)}, u32[]{:S(2)}) async-start(bf16[16,144,128]{2,1,0:T(8,128)(2,1)} %broadcast_in_dim.16), calls=%async_computation.1 | async-start | bytes 1179648 | tf_op jit(solution)/shard_map/all_to_all | solution.py:327
  94.0 10.8 %attention_backward.1 = (bf16[256,2048]{1,0:T(8,128)(2,1)}, bf16[256,1024]{1,0:T(8,128)(2,1)}, bf16[256,1024]{1,0:T(8,128)(2,1)}) custom-call(s32[9]{0:T(128)} %pad_add_fusion.place_ref, bf16[256,2048]{1,0:T(8,128)(2,1)} %q_ref.3, bf16[256,1024]{1,0:T(8,128)(2,1)} %k_ref.3, bf16[256,1024]{1,0:T(8,128)(2,1)} %v_ref.3, ...), custom_call_target="tpu_custom_call" | custom-call | flops 230000000 | bytes 9437184 | tf_op jit(solution)/shard_map/attention_backward/pallas_call | solution.py:148
  104.8 2.4 %fusion = bf16[1,128,2304]{2,1,0:T(8,128)(2,1)} fusion(bf16[128,2304]{1,0:T(8,128)(2,1)} %collective-permute-done.17, bf16[128,2304]{1,0:T(8,128)(2,1)} %collective-permute-done.16, bf16[128,2304]{1,0:T(8,128)(2,1)S(1)} %collective-permute-done.15, bf16[128,2304]{1,0:T(8,128)(2,1)S(1)} %copy-done.7), kind=kLoop, calls=%fused_computation.6 | loop fusion | flops 2359296 | bytes 2949120 | tf_op jit(solution)/shard_map/broadcast_in_dim | solution.py:394
  107.3 1.3 %add_convert_fusion = bf16[256,2304]{1,0:T(8,128)(2,1)} fusion(bf16[256,2304]{1,0:T(8,128)(2,1)S(1)} %collective-permute-done.10, bf16[256,2304]{1,0:T(8,128)(2,1)S(1)} %copy-done.3), kind=kLoop, calls=%fused_computation | loop fusion | flops 2359296 | bytes 3538944 | tf_op jit(solution)/shard_map/convert_element_type | solution.py:298
  108.6 2.7 %all-to-all-done.1 = bf16[16,144,128]{2,1,0:T(8,128)(2,1)S(1)} async-done(((bf16[16,144,128]{2,1,0:T(8,128)(2,1)}), bf16[16,144,128]{2,1,0:T(8,128)(2,1)S(1)}, u32[]{:S(2)}, u32[]{:S(2)}) %all-to-all-start.1) | async-done | bytes 589856 | tf_op jit(solution)/shard_map/all_to_all | solution.py:327
  112.1 3.8 %outer_update.1 = (f32[128,2304]{1,0:T(8,128)}, bf16[128,2304]{1,0:T(8,128)(2,1)}) custom-call(bf16[2304,128]{1,0:T(8,128)(2,1)} %bitcast.20, f32[128,2304]{1,0:T(8,128)} %anchor_ref.1, bf16[128,2304]{1,0:T(8,128)(2,1)} %bitcast.21), custom_call_target="tpu_custom_call" | custom-call | flops 69000000 | bytes 4194304 | tf_op jit(solution)/shard_map/outer_update/pallas_call | solution.py:329
  (58 shorter events, 11.4 us)
Async XLA Ops:
  0.6 24.0 %collective-permute-start = (bf16[256,2304]{1,0:T(8,128)(2,1)}, bf16[256,2304]{1,0:T(8,128)(2,1)S(1)}, u32[]{:S(2)}, u32[]{:S(2)}) collective-permute-start(bf16[256,2304]{1,0:T(8,128)(2,1)} %g0_ref.3), channel_id=1, source_target_pairs={{0,1},{1,0},{2,3},{3,2},{4,5},{5,4},{6,7},{7,6},{8,9},{9,8},{10,11... | collective-permute-start | bytes 3538952 | tf_op jit(solution)/shard_map/ppermute | solution.py:291
  0.7 16.3 %collective-permute-start.1 = (bf16[128,2304]{1,0:T(8,128)(2,1)}, bf16[128,2304]{1,0:T(8,128)(2,1)S(1)}, u32[]{:S(2)}, u32[]{:S(2)}) collective-permute-start(bf16[128,2304]{1,0:T(8,128)(2,1)} %bitcast.22), channel_id=1, source_target_pairs={{0,6},{1,7},{2,0},{3,1},{4,2},{5,3},{6,4},{7,5},{8,14},{9,15},{10,... | collective-permute-start | bytes 1769480 | tf_op jit(solution)/shard_map/ppermute | solution.py:283
  3.6 16.8 %collective-permute-start.2 = (bf16[128,2304]{1,0:T(8,128)(2,1)}, bf16[128,2304]{1,0:T(8,128)(2,1)S(1)}, u32[]{:S(2)}, u32[]{:S(2)}) collective-permute-start(bf16[128,2304]{1,0:T(8,128)(2,1)} %bitcast.23), channel_id=1, source_target_pairs={{0,2},{1,3},{2,4},{3,5},{4,6},{5,7},{6,0},{7,1},{8,10},{9,11},{10,... | collective-permute-start | bytes 1769480 | tf_op jit(solution)/shard_map/ppermute | solution.py:279
  3.6 16.8 %collective-permute-start.3 = (bf16[128,2304]{1,0:T(8,128)(2,1)}, bf16[128,2304]{1,0:T(8,128)(2,1)}, u32[]{:S(2)}, u32[]{:S(2)}) collective-permute-start(bf16[128,2304]{1,0:T(8,128)(2,1)} %bitcast.24), channel_id=1, source_target_pairs={{0,8},{1,9},{2,10},{3,11},{4,12},{5,13},{6,14},{7,15},{8,0},{9,1},... | collective-permute-start | bytes 1769480 | tf_op jit(solution)/shard_map/ppermute | solution.py:287
  20.4 19.5 %copy-start.10 = (bf16[128,2304]{1,0:T(8,128)(2,1)}, bf16[128,2304]{1,0:T(8,128)(2,1)S(1)}, u32[]{:S(2)}) copy-start(bf16[128,2304]{1,0:T(8,128)(2,1)S(1)} %collective-permute-done.2.refs_2_) | copy-start | bytes 1769476
  20.4 14.9 %collective-permute-start.5 = (bf16[128,2304]{1,0:T(8,128)(2,1)}, bf16[128,2304]{1,0:T(8,128)(2,1)}, u32[]{:S(2)}, u32[]{:S(2)}) collective-permute-start(bf16[128,2304]{1,0:T(8,128)(2,1)} %collective-permute-done.3.refs_3_), channel_id=1, source_target_pairs={{0,6},{1,7},{2,0},{3,1},{4,2},{5,3},{6,4},{7,5},{8,14},{9,15},{10,... | collective-permute-start | bytes 1769480 | tf_op jit(solution)/shard_map/ppermute | solution.py:283
  22.4 17.5 %collective-permute-start.6 = (bf16[128,2304]{1,0:T(8,128)(2,1)S(1)}, bf16[128,2304]{1,0:T(8,128)(2,1)S(1)}, u32[]{:S(2)}, u32[]{:S(2)}) collective-permute-start(bf16[128,2304]{1,0:T(8,128)(2,1)S(1)} %collective-permute-done.2.refs_2_), channel_id=1, source_target_pairs={{0,2},{1,3},{2,4},{3,5},{4,6},{5,7},{6,0},{7,1},{8,10},{9,11},{10,... | collective-permute-start | bytes 1769480 | tf_op jit(solution)/shard_map/ppermute | solution.py:279
  22.4 19.3 %copy-start.4 = (f32[1,128,2304]{2,1,0:T(8,128)S(1)}, f32[1,128,2304]{2,1,0:T(8,128)}, u32[]{:S(2)}) copy-start(f32[1,128,2304]{2,1,0:T(8,128)} %param.16) | copy-start | bytes 3538948
  22.4 2.2 %collective-permute-start.4 = (bf16[256,1024]{1,0:T(8,128)(2,1)}, bf16[256,1024]{1,0:T(8,128)(2,1)S(1)}, u32[]{:S(2)}, u32[]{:S(2)}) collective-permute-start(bf16[256,1024]{1,0:T(8,128)(2,1)} %get-tuple-element.51), channel_id=1, source_target_pairs={{0,1},{1,0},{2,3},{3,2},{4,5},{5,4},{6,7},{7,6},{8,9},{9,8},{10,11... | collective-permute-start | bytes 1572872 | tf_op jit(solution)/shard_map/ppermute | solution.py:291
  22.5 31.0 %collective-permute-start.8 = (bf16[128,2304]{1,0:T(8,128)(2,1)}, bf16[128,2304]{1,0:T(8,128)(2,1)}, u32[]{:S(2)}, u32[]{:S(2)}) collective-permute-start(bf16[128,2304]{1,0:T(8,128)(2,1)} %collective-permute-done.3.refs_3_), channel_id=1, source_target_pairs={{0,2},{1,3},{2,4},{3,5},{4,6},{5,7},{6,0},{7,1},{8,10},{9,11},{10,... | collective-permute-start | bytes 1769480 | tf_op jit(solution)/shard_map/ppermute | solution.py:279
  39.9 14.7 %collective-permute-start.7 = (bf16[128,2304]{1,0:T(8,128)(2,1)}, bf16[128,2304]{1,0:T(8,128)(2,1)}, u32[]{:S(2)}, u32[]{:S(2)}) collective-permute-start(bf16[128,2304]{1,0:T(8,128)(2,1)} %collective-permute-done.5.refs_4_), channel_id=1, source_target_pairs={{0,6},{1,7},{2,0},{3,1},{4,2},{5,3},{6,4},{7,5},{8,14},{9,15},{10,... | collective-permute-start | bytes 1769480 | tf_op jit(solution)/shard_map/ppermute | solution.py:283
  39.9 15.6 %collective-permute-start.9 = (bf16[128,2304]{1,0:T(8,128)(2,1)}, bf16[128,2304]{1,0:T(8,128)(2,1)S(1)}, u32[]{:S(2)}, u32[]{:S(2)}) collective-permute-start(bf16[128,2304]{1,0:T(8,128)(2,1)} %get-tuple-element.63), channel_id=1, source_target_pairs={{0,8},{1,9},{2,10},{3,11},{4,12},{5,13},{6,14},{7,15},{8,0},{9,1},... | collective-permute-start | bytes 1769480 | tf_op jit(solution)/shard_map/ppermute | solution.py:287
  41.7 13.8 %copy-start.6 = (bf16[128,2304]{1,0:T(8,128)(2,1)S(1)}, bf16[128,2304]{1,0:T(8,128)(2,1)}, u32[]{:S(2)}) copy-start(bf16[128,2304]{1,0:T(8,128)(2,1)} %get-tuple-element.62) | copy-start | bytes 1769476
  42.9 31.5 %all-to-all-start = ((bf16[16,144,128]{2,1,0:T(8,128)(2,1)}), bf16[16,144,128]{2,1,0:T(8,128)(2,1)S(1)}, u32[]{:S(2)}, u32[]{:S(2)}) async-start(bf16[16,144,128]{2,1,0:T(8,128)(2,1)} %bitcast.3), calls=%async_computation | async-start | bytes 1179648 | tf_op jit(solution)/shard_map/all_to_all | solution.py:317
  53.5 23.9 %collective-permute-start.11 = (bf16[128,2304]{1,0:T(8,128)(2,1)}, bf16[128,2304]{1,0:T(8,128)(2,1)}, u32[]{:S(2)}, u32[]{:S(2)}) collective-permute-start(bf16[128,2304]{1,0:T(8,128)(2,1)} %get-tuple-element.70), channel_id=1, source_target_pairs={{0,8},{1,9},{2,10},{3,11},{4,12},{5,13},{6,14},{7,15},{8,0},{9,1},... | collective-permute-start | bytes 1769480 | tf_op jit(solution)/shard_map/ppermute | solution.py:287
  54.6 20.5 %collective-permute-start.13 = (bf16[128,2304]{1,0:T(8,128)(2,1)}, bf16[128,2304]{1,0:T(8,128)(2,1)S(1)}, u32[]{:S(2)}, u32[]{:S(2)}) collective-permute-start(bf16[128,2304]{1,0:T(8,128)(2,1)} %get-tuple-element.73), channel_id=1, source_target_pairs={{0,6},{1,7},{2,0},{3,1},{4,2},{5,3},{6,4},{7,5},{8,14},{9,15},{10,... | collective-permute-start | bytes 1769480 | tf_op jit(solution)/shard_map/ppermute | solution.py:283
  55.6 18.8 %copy-start.12 = (f32[128,144]{0,1:T(8,128)S(1)}, f32[128,144]{0,1:T(8,128)}, u32[]{:S(2)}) copy-start(f32[128,144]{0,1:T(8,128)} %param.18) | copy-start | bytes 221188
  55.7 21.7 %collective-permute-start.12 = (bf16[128,2304]{1,0:T(8,128)(2,1)S(1)}, bf16[128,2304]{1,0:T(8,128)(2,1)S(1)}, u32[]{:S(2)}, u32[]{:S(2)}) collective-permute-start(bf16[128,2304]{1,0:T(8,128)(2,1)S(1)} %add_convert_fusion.4), channel_id=1, source_target_pairs={{0,2},{1,3},{2,4},{3,5},{4,6},{5,7},{6,0},{7,1},{8,10},{9,11},{10,... | collective-permute-start | bytes 1769480 | tf_op jit(solution)/shard_map/ppermute | solution.py:279
  79.6 25.2 %collective-permute-start.15 = (bf16[128,2304]{1,0:T(8,128)(2,1)}, bf16[128,2304]{1,0:T(8,128)(2,1)S(1)}, u32[]{:S(2)}, u32[]{:S(2)}) collective-permute-start(bf16[128,2304]{1,0:T(8,128)(2,1)} %get-tuple-element.84), channel_id=1, source_target_pairs={{0,6},{1,7},{2,0},{3,1},{4,2},{5,3},{6,4},{7,5},{8,14},{9,15},{10,... | collective-permute-start | bytes 1769480 | tf_op jit(solution)/shard_map/ppermute | solution.py:283
  79.9 24.9 %collective-permute-start.17 = (bf16[128,2304]{1,0:T(8,128)(2,1)S(1)}, bf16[128,2304]{1,0:T(8,128)(2,1)}, u32[]{:S(2)}, u32[]{:S(2)}) collective-permute-start(bf16[128,2304]{1,0:T(8,128)(2,1)S(1)} %add_convert_fusion.2), channel_id=1, source_target_pairs={{0,8},{1,9},{2,10},{3,11},{4,12},{5,13},{6,14},{7,15},{8,0},{9,1},... | collective-permute-start | bytes 1769480 | tf_op jit(solution)/shard_map/ppermute | solution.py:287
  81.2 23.6 %collective-permute-start.16 = (bf16[128,2304]{1,0:T(8,128)(2,1)S(1)}, bf16[128,2304]{1,0:T(8,128)(2,1)}, u32[]{:S(2)}, u32[]{:S(2)}) collective-permute-start(bf16[128,2304]{1,0:T(8,128)(2,1)S(1)} %add_convert_fusion.3), channel_id=1, source_target_pairs={{0,2},{1,3},{2,4},{3,5},{4,6},{5,7},{6,0},{7,1},{8,10},{9,11},{10,... | collective-permute-start | bytes 1769480 | tf_op jit(solution)/shard_map/ppermute | solution.py:279
  82.9 11.1 %collective-permute-start.14 = (bf16[256,1024]{1,0:T(8,128)(2,1)}, bf16[256,1024]{1,0:T(8,128)(2,1)}, u32[]{:S(2)}, u32[]{:S(2)}) collective-permute-start(bf16[256,1024]{1,0:T(8,128)(2,1)} %get-tuple-element.77), channel_id=1, source_target_pairs={{0,1},{1,0},{2,3},{3,2},{4,5},{5,4},{6,7},{7,6},{8,9},{9,8},{10,11... | collective-permute-start | bytes 1572872 | tf_op jit(solution)/shard_map/ppermute | solution.py:291
  82.9 24.4 %collective-permute-start.10 = (bf16[256,2304]{1,0:T(8,128)(2,1)}, bf16[256,2304]{1,0:T(8,128)(2,1)S(1)}, u32[]{:S(2)}, u32[]{:S(2)}) collective-permute-start(bf16[256,2304]{1,0:T(8,128)(2,1)} %get-tuple-element.67), channel_id=1, source_target_pairs={{0,1},{1,0},{2,3},{3,2},{4,5},{5,4},{6,7},{7,6},{8,9},{9,8},{10,11... | collective-permute-start | bytes 3538952 | tf_op jit(solution)/shard_map/ppermute | solution.py:291
  83.4 27.9 %all-to-all-start.1 = ((bf16[16,144,128]{2,1,0:T(8,128)(2,1)}), bf16[16,144,128]{2,1,0:T(8,128)(2,1)S(1)}, u32[]{:S(2)}, u32[]{:S(2)}) async-start(bf16[16,144,128]{2,1,0:T(8,128)(2,1)} %broadcast_in_dim.16), calls=%async_computation.1 | async-start | bytes 1179648 | tf_op jit(solution)/shard_map/all_to_all | solution.py:327
  (9 other events, 32.7 us)

commit v4 on v3

--- a/solution.py
+++ b/solution.py
@@ -312,9 +312,8 @@
     return shares.transpose(1, 2, 0)
 
 
-def outer_share(packed, momentum):
+def outer_share(shares, momentum):
     replicas = lax.axis_size("rep")
-    shares = lax.all_to_all(packed, "rep", 0, 0, tiled=False)
     mean_share = jnp.sum(shares.astype(jnp.float32), axis=0).T / replicas
     momentum_new = outer_moment * momentum + mean_share
     step_share = (outer_moment * momentum_new + mean_share).astype(jnp.bfloat16).T
@@ -324,7 +323,7 @@
 def outer_update(steps, anchor, local):
     rows, width = anchor.shape
     tile = width // COLUMN_TILES
-    steps = lax.all_to_all(steps, "rep", 0, 0, tiled=False).reshape(width, rows)
+    steps = steps.reshape(width, rows)
     part = pl.BlockSpec((rows, tile), lambda j: (0, j))
     return pl.pallas_call(
         update_kernel,
@@ -359,6 +358,9 @@
     w3 = to_right(own_rows)
     w1 = to_left(own_rows)
     w4 = to_far(own_rows)
+    packed = packed_shares(pseudo_grad[0])
+    query_states, packed = lax.optimization_barrier((query_states, packed))
+    shares = lax.all_to_all(packed, "rep", 0, 0, tiled=False)
     mixed_own, mixed_other = forward(place, query_states, key_states, value_states)
     mixed_peer = to_peer(mixed_other)
     w1, w3, w4, mixed_own = lax.optimization_barrier((w1, w3, w4, mixed_own))
@@ -369,15 +371,14 @@
     d0, d1, d3, d4, d5, d2, d7, d6 = weight_grad_pieces(
         mixed_own, mixed_peer, output_grad, grad_peer
     )
-    w5, w2, d6 = lax.optimization_barrier((w5, w2, d6))
+    w5, w2, d6, shares = lax.optimization_barrier((w5, w2, d6, shares))
     w6 = to_left(w5)
     r2 = to_far(d6)
     r1f = to_far(d5)
     w6, d7 = lax.optimization_barrier((w6, d7))
     r4 = to_left(d7)
-    d0, pseudo_grad = lax.optimization_barrier((d0, pseudo_grad))
-    momentum_new, steps = outer_share(packed_shares(pseudo_grad[0]), momentum)
-    w7, d2 = lax.optimization_barrier((w7, d2))
+    momentum_new, steps = outer_share(shares, momentum)
+    w7, d2, _ = lax.optimization_barrier((w7, d2, steps))
     s2 = added(d2, r2)
     w6, w7, s2 = lax.optimization_barrier((w6, w7, s2))
     r1 = to_right(s2)
@@ -386,12 +387,14 @@
     )
     s1 = added(d1, r1f, r1)
     s4 = added(d4, r4)
-    grad_mixed, s1, s4, steps = lax.optimization_barrier((grad_mixed, s1, s4, steps))
+    grad_mixed, s1, s4 = lax.optimization_barrier((grad_mixed, s1, s4))
     d3, s4 = lax.optimization_barrier((d3, s4))
     from_right = to_left(d3)
     from_left = to_right(s1)
     from_far = to_far(s4)
     weight_grad = added(d0, from_right, from_left, from_far)[None]
+    steps = lax.all_to_all(steps, "rep", 0, 0, tiled=False)
+    grad_mixed, steps = lax.optimization_barrier((grad_mixed, steps))
     grad_query, grad_key, grad_value = backward(
         place, query_states, key_states, value_states, grad_mixed, to_peer(grad_send)
     )

time: 118 us -> 111 us (0.941); the launches traced: 116 us -> 111 us
  waiting for transfers between devices: 25.9 us -> 17.3 us
  local copies, waits for them, and re-layouts: 4.66 us -> 7.51 us
  starting transfers between devices: 36.5 us -> 37.7 us
    all_to_all x2, waiting for transfers between devices: 8.62 us -> 0.01 us  [the longest x1 0.01 us: on_device(): shares = lax.all_to_all(packed, 'rep', 0, 0, tiled=False)]
    ppermute x5, waiting for transfers between devices: 7.97 us -> 13.5 us  [to_right(): return lax.ppermute(array, 'fsdp', shift(0, 1, 0))]
    unnamed x26 -> x29, local copies, waits for them, and re-layouts: 2.65 us -> 6.62 us
    ppermute x5, starting transfers between devices: 5.28 us -> 9.03 us  [to_left(): return lax.ppermute(array, 'fsdp', shift(0, -1, 0))]
    ppermute x4, waiting for transfers between devices: 2.98 us -> 0.01 us  [to_far(): return lax.ppermute(array, 'fsdp', shift(1, 0, 0))]
    ppermute x5, waiting for transfers between devices: 4.26 us -> 1.66 us  [to_left(): return lax.ppermute(array, 'fsdp', shift(0, -1, 0))]
  transfers between devices with their start and end apart: 20 -> 20, of which waited for: 9 -> 4; matrix products, arithmetic and copies ran while one was open for 6% -> 7% of each run, Pallas kernels for 32% -> 37%
where the time goes in v4:
time: 111 us
  Pallas kernels  40.7 us (37%)
  starting transfers between devices  37.7 us (34%)
  waiting for transfers between devices  17.3 us (16%)
  local copies, waits for them, and re-layouts  7.51 us (7%)
  other arithmetic  6.4 us (6%)
    ppermute x5, waiting for transfers between devices, to_right(): return lax.ppermute(array, 'fsdp', shift(0, 1, 0))  13.5 us
    pallas_call x1, Pallas kernels, project(): pl.pallas_call(project_kernel, grid=(COLUMN_TILES,), in_specs=[part, part...  11.3 us
    pallas_call x1, Pallas kernels, backward(): pl.pallas_call(backward_kernel, grid_spec=pltpu.PrefetchScalarGridSpec(nu...  10.8 us
    all_to_all x1, starting transfers between devices, on_device(): shares = lax.all_to_all(packed, 'rep', 0, 0, tiled=False)  10.7 us
    all_to_all x1, starting transfers between devices, on_device(): steps = lax.all_to_all(steps, 'rep', 0, 0, tiled=False)  9.63 us
    ppermute x5, starting transfers between devices, to_left(): return lax.ppermute(array, 'fsdp', shift(0, -1, 0))  9.03 us
    pallas_call x1, Pallas kernels, forward(): pl.pallas_call(forward_kernel, grid_spec=pltpu.PrefetchScalarGridSpec(num...  8.63 us
    unnamed x29, local copies, waits for them, and re-layouts  6.62 us
  transfers between devices with their start and end apart: 20, of which 4 were waited for; matrix products, arithmetic and copies ran while one was open for 7% of the time, Pallas kernels for 37%

profile of v4, /device:TPU:8, one launch (start us, length us, event | category | flops | bytes accessed | tf_op | source)
XLA Modules:
  0.0 110.5 jit_solution(8753193720462478891)
XLA Ops:
  0.8 2.8 %collective-permute-start.1 = (bf16[128,2304]{1,0:T(8,128)(2,1)}, bf16[128,2304]{1,0:T(8,128)(2,1)S(1)}, u32[]{:S(2)}, u32[]{:S(2)}) collective-permute-start(bf16[128,2304]{1,0:T(8,128)(2,1)} %bitcast.22), channel_id=1, source_target_pairs={{0,6},{1,7},{2,0},{3,1},{4,2},{5,3},{6,4},{7,5},{8,14},{9,15},{10,... | collective-permute-start | bytes 1769480 | tf_op jit(solution)/shard_map/ppermute | solution.py:283
  3.6 1.9 %collective-permute-start.3 = (bf16[128,2304]{1,0:T(8,128)(2,1)}, bf16[128,2304]{1,0:T(8,128)(2,1)S(1)}, u32[]{:S(2)}, u32[]{:S(2)}) collective-permute-start(bf16[128,2304]{1,0:T(8,128)(2,1)} %bitcast.24), channel_id=1, source_target_pairs={{0,8},{1,9},{2,10},{3,11},{4,12},{5,13},{6,14},{7,15},{8,0},{9,1},... | collective-permute-start | bytes 1769480 | tf_op jit(solution)/shard_map/ppermute | solution.py:287
  5.5 2.3 %copy.19 = bf16[1,128,2304]{1,2,0:T(8,128)(2,1)} copy(f32[1,128,2304]{2,1,0:T(8,128)} %param.16) | data formatting | bytes 1769472 | tf_op args[5]
  7.8 10.7 %all-to-all-start = ((bf16[16,144,128]{2,1,0:T(8,128)(2,1)}), bf16[16,144,128]{2,1,0:T(8,128)(2,1)S(1)}, u32[]{:S(2)}, u32[]{:S(2)}) async-start(bf16[16,144,128]{2,1,0:T(8,128)(2,1)} %bitcast.3), calls=%async_computation | async-start | bytes 1179648 | tf_op jit(solution)/shard_map/all_to_all | solution.py:363
  19.2 8.6 %attention_forward.1 = (bf16[256,1024]{1,0:T(8,128)(2,1)}, bf16[256,1024]{1,0:T(8,128)(2,1)}) custom-call(s32[9]{0:T(128)} %pad_add_fusion.place_ref, bf16[256,2048]{1,0:T(8,128)(2,1)} %q_ref.1, bf16[256,1024]{1,0:T(8,128)(2,1)} %k_ref.3, bf16[256,1024]{1,0:T(8,128)(2,1)} %v_ref.3), custom_call_target="tpu_custom_call" | custom-call | flops 161000000 | bytes 4194304 | tf_op jit(solution)/shard_map/attention_forward/pallas_call | solution.py:102
  27.9 3.3 %collective-permute-start.5 = (bf16[128,2304]{1,0:T(8,128)(2,1)S(1)}, bf16[128,2304]{1,0:T(8,128)(2,1)}, u32[]{:S(2)}, u32[]{:S(2)}) collective-permute-start(bf16[128,2304]{1,0:T(8,128)(2,1)S(1)} %collective-permute-done.3.refs_3_), channel_id=1, source_target_pairs={{0,6},{1,7},{2,0},{3,1},{4,2},{5,3},{6,4},{7,5},{8,14},{9,15},{10,... | collective-permute-start | bytes 1769480 | tf_op jit(solution)/shard_map/ppermute | solution.py:283
  31.2 2.1 %collective-permute-done.4.m1_ref = bf16[256,1024]{1,0:T(8,128)(2,1)S(1)} collective-permute-done((bf16[256,1024]{1,0:T(8,128)(2,1)}, bf16[256,1024]{1,0:T(8,128)(2,1)S(1)}, u32[]{:S(2)}, u32[]{:S(2)}) %collective-permute-start.4) | collective-permute-done | bytes 524320 | tf_op jit(solution)/shard_map/ppermute | solution.py:291
  34.1 1.0 copy-done
  35.1 6.2 %weight_grad_partial.1 = (bf16[128,2304]{1,0:T(8,128)(2,1)}, bf16[128,2304]{1,0:T(8,128)(2,1)}, bf16[128,2304]{1,0:T(8,128)(2,1)}, bf16[128,2304]{1,0:T(8,128)(2...) custom-call(bf16[256,1024]{1,0:T(8,128)(2,1)} %get-tuple-element.53., ...), custom_call_target="tpu_custom_call" | custom-call | flops 115000000 | bytes 8388608 | tf_op jit(solution)/shard_map/weight_grad_partial/pallas_call | solution.py:197
  41.3 1.6 %collective-permute-done.5.refs_4_ = bf16[128,2304]{1,0:T(8,128)(2,1)} collective-permute-done((bf16[128,2304]{1,0:T(8,128)(2,1)S(1)}, bf16[128,2304]{1,0:T(8,128)(2,1)}, u32[]{:S(2)}, u32[]{:S(2)}) %collective-permute-start.5) | collective-permute-done | bytes 589856 | tf_op jit(solution)/shard_map/ppermute | solution.py:283
  43.0 5.8 %collective-permute-done.6.refs_5_ = bf16[128,2304]{1,0:T(8,128)(2,1)} collective-permute-done((bf16[128,2304]{1,0:T(8,128)(2,1)S(1)}, bf16[128,2304]{1,0:T(8,128)(2,1)}, u32[]{:S(2)}, u32[]{:S(2)}) %collective-permute-start.6) | collective-permute-done | bytes 589856 | tf_op jit(solution)/shard_map/ppermute | solution.py:279
  48.8 1.0 collective-permute-start.9
  49.9 1.5 %fusion.2 = (bf16[144,128]{1,0:T(8,128)(2,1)S(1)}, f32[128,144]{0,1:T(8,128)}) fusion(f32[144,128]{1,0:T(8,128)S(1)} %convert_reduce_fusion, f32[128,144]{0,1:T(8,128)} %param.18), kind=kLoop, calls=%fused_computation.10 | loop fusion | flops 110592 | bytes 258048 | tf_op jit(solution)/shard_map/transpose | solution.py:319
  51.4 7.7 %collective-permute-done.8.refs_6_ = bf16[128,2304]{1,0:T(8,128)(2,1)} collective-permute-done((bf16[128,2304]{1,0:T(8,128)(2,1)S(1)}, bf16[128,2304]{1,0:T(8,128)(2,1)}, u32[]{:S(2)}, u32[]{:S(2)}) %collective-permute-start.8) | collective-permute-done | bytes 589856 | tf_op jit(solution)/shard_map/ppermute | solution.py:279
  62.0 1.2 %collective-permute-start.12 = (bf16[128,2304]{1,0:T(8,128)(2,1)S(1)}, bf16[128,2304]{1,0:T(8,128)(2,1)S(1)}, u32[]{:S(2)}, u32[]{:S(2)}) collective-permute-start(bf16[128,2304]{1,0:T(8,128)(2,1)S(1)} %add_convert_fusion.4), channel_id=1, source_target_pairs={{0,2},{1,3},{2,4},{3,5},{4,6},{5,7},{6,0},{7,1},{8,10},{9,11},{10,... | collective-permute-start | bytes 1769480 | tf_op jit(solution)/shard_map/ppermute | solution.py:279
  63.2 9.6 %all-to-all-start.1 = ((bf16[16,144,128]{2,1,0:T(8,128)(2,1)}), bf16[16,144,128]{2,1,0:T(8,128)(2,1)S(1)}, u32[]{:S(2)}, u32[]{:S(2)}) async-start(bf16[16,144,128]{2,1,0:T(8,128)(2,1)} %broadcast_in_dim.16), calls=%async_computation.1 | async-start | bytes 1179648 | tf_op jit(solution)/shard_map/all_to_all | solution.py:396
  72.8 2.4 %collective-permute-start.13 = (bf16[128,2304]{1,0:T(8,128)(2,1)}, bf16[128,2304]{1,0:T(8,128)(2,1)S(1)}, u32[]{:S(2)}, u32[]{:S(2)}) collective-permute-start(bf16[128,2304]{1,0:T(8,128)(2,1)} %get-tuple-element.78), channel_id=1, source_target_pairs={{0,6},{1,7},{2,0},{3,1},{4,2},{5,3},{6,4},{7,5},{8,14},{9,15},{10,... | collective-permute-start | bytes 1769480 | tf_op jit(solution)/shard_map/ppermute | solution.py:283
  75.2 11.3 %project.1 = (bf16[256,1024]{1,0:T(8,128)(2,1)}, bf16[256,1024]{1,0:T(8,128)(2,1)}, bf16[256,2304]{1,0:T(8,128)(2,1)}, bf16[256,2304]{1,0:T(8,128)(2,1)}) custom-call(bf16[256,2304]{1,0:T(8,128)(2,1)} %g0_ref.3, bf16[256,2304]{1,0:T(8,128)(2,1)} %copy-done, bf16[256,1024]{1,0:T(8,128)(2,1)} %get-tuple-element.53.m0_ref, bf16[256,1024]{1,0:T(8,128)(2,1)} %copy-done.2, ...), custom_call_target="tpu_custom_call" | custom-call | flops 253000000 | bytes 14680064 | tf_op jit(solution)/shard_map/project/pallas_call | solution.py:243
  88.8 1.0 collective-permute-start.17
  89.8 1.6 %collective-permute-start.16 = (bf16[128,2304]{1,0:T(8,128)(2,1)S(1)}, bf16[128,2304]{1,0:T(8,128)(2,1)}, u32[]{:S(2)}, u32[]{:S(2)}) collective-permute-start(bf16[128,2304]{1,0:T(8,128)(2,1)S(1)} %add_convert_fusion.3), channel_id=1, source_target_pairs={{0,2},{1,3},{2,4},{3,5},{4,6},{5,7},{6,0},{7,1},{8,10},{9,11},{10,... | collective-permute-start | bytes 1769480 | tf_op jit(solution)/shard_map/ppermute | solution.py:279
  92.2 3.8 %outer_update.1 = (f32[128,2304]{1,0:T(8,128)}, bf16[128,2304]{1,0:T(8,128)(2,1)}) custom-call(bf16[2304,128]{1,0:T(8,128)(2,1)} %bitcast.20, f32[128,2304]{1,0:T(8,128)} %anchor_ref.1, bf16[128,2304]{1,0:T(8,128)(2,1)} %bitcast.21), custom_call_target="tpu_custom_call" | custom-call | flops 69000000 | bytes 4194304 | tf_op jit(solution)/shard_map/outer_update/pallas_call | solution.py:328
  96.1 10.8 %attention_backward.1 = (bf16[256,2048]{1,0:T(8,128)(2,1)}, bf16[256,1024]{1,0:T(8,128)(2,1)}, bf16[256,1024]{1,0:T(8,128)(2,1)}) custom-call(s32[9]{0:T(128)} %pad_add_fusion.place_ref, bf16[256,2048]{1,0:T(8,128)(2,1)} %q_ref.1, bf16[256,1024]{1,0:T(8,128)(2,1)} %k_ref.3, bf16[256,1024]{1,0:T(8,128)(2,1)} %v_ref.3, ...), custom_call_target="tpu_custom_call" | custom-call | flops 230000000 | bytes 9437184 | tf_op jit(solution)/shard_map/attention_backward/pallas_call | solution.py:148
  106.9 1.3 %add_convert_fusion = bf16[256,2304]{1,0:T(8,128)(2,1)} fusion(bf16[256,2304]{1,0:T(8,128)(2,1)S(1)} %collective-permute-done.10, bf16[256,2304]{1,0:T(8,128)(2,1)S(1)} %copy-done.3), kind=kLoop, calls=%fused_computation | loop fusion | flops 2359296 | bytes 3538944 | tf_op jit(solution)/shard_map/convert_element_type | solution.py:298
  108.2 2.3 %fusion = bf16[1,128,2304]{2,1,0:T(8,128)(2,1)} fusion(bf16[128,2304]{1,0:T(8,128)(2,1)} %collective-permute-done.17, bf16[128,2304]{1,0:T(8,128)(2,1)} %collective-permute-done.16, bf16[128,2304]{1,0:T(8,128)(2,1)S(1)} %collective-permute-done.15, bf16[128,2304]{1,0:T(8,128)(2,1)S(1)} %copy-done.6), kind=kLoop, calls=%fused_computation.6 | loop fusion | flops 2359296 | bytes 2949120 | tf_op jit(solution)/shard_map/broadcast_in_dim | solution.py:395
  (60 shorter events, 7.6 us)
Async XLA Ops:
  0.6 32.7 %collective-permute-start = (bf16[256,2304]{1,0:T(8,128)(2,1)}, bf16[256,2304]{1,0:T(8,128)(2,1)S(1)}, u32[]{:S(2)}, u32[]{:S(2)}) collective-permute-start(bf16[256,2304]{1,0:T(8,128)(2,1)} %g0_ref.3), channel_id=1, source_target_pairs={{0,1},{1,0},{2,3},{3,2},{4,5},{5,4},{6,7},{7,6},{8,9},{9,8},{10,11... | collective-permute-start | bytes 3538952 | tf_op jit(solution)/shard_map/ppermute | solution.py:291
  0.7 17.8 %copy-start.12 = (s32[8]{0:T(128)S(1)}, s32[8]{0:T(128)}, u32[]{:S(2)}) copy-start(s32[8]{0:T(128)} %constant.73.clone) | copy-start | bytes 100
  0.8 27.1 %collective-permute-start.1 = (bf16[128,2304]{1,0:T(8,128)(2,1)}, bf16[128,2304]{1,0:T(8,128)(2,1)S(1)}, u32[]{:S(2)}, u32[]{:S(2)}) collective-permute-start(bf16[128,2304]{1,0:T(8,128)(2,1)} %bitcast.22), channel_id=1, source_target_pairs={{0,6},{1,7},{2,0},{3,1},{4,2},{5,3},{6,4},{7,5},{8,14},{9,15},{10,... | collective-permute-start | bytes 1769480 | tf_op jit(solution)/shard_map/ppermute | solution.py:283
  3.6 24.2 %collective-permute-start.2 = (bf16[128,2304]{1,0:T(8,128)(2,1)}, bf16[128,2304]{1,0:T(8,128)(2,1)S(1)}, u32[]{:S(2)}, u32[]{:S(2)}) collective-permute-start(bf16[128,2304]{1,0:T(8,128)(2,1)} %bitcast.23), channel_id=1, source_target_pairs={{0,2},{1,3},{2,4},{3,5},{4,6},{5,7},{6,0},{7,1},{8,10},{9,11},{10,... | collective-permute-start | bytes 1769480 | tf_op jit(solution)/shard_map/ppermute | solution.py:279
  3.6 24.3 %collective-permute-start.3 = (bf16[128,2304]{1,0:T(8,128)(2,1)}, bf16[128,2304]{1,0:T(8,128)(2,1)S(1)}, u32[]{:S(2)}, u32[]{:S(2)}) collective-permute-start(bf16[128,2304]{1,0:T(8,128)(2,1)} %bitcast.24), channel_id=1, source_target_pairs={{0,8},{1,9},{2,10},{3,11},{4,12},{5,13},{6,14},{7,15},{8,0},{9,1},... | collective-permute-start | bytes 1769480 | tf_op jit(solution)/shard_map/ppermute | solution.py:287
  7.8 33.5 %all-to-all-start = ((bf16[16,144,128]{2,1,0:T(8,128)(2,1)}), bf16[16,144,128]{2,1,0:T(8,128)(2,1)S(1)}, u32[]{:S(2)}, u32[]{:S(2)}) async-start(bf16[16,144,128]{2,1,0:T(8,128)(2,1)} %bitcast.3), calls=%async_computation | async-start | bytes 1179648 | tf_op jit(solution)/shard_map/all_to_all | solution.py:363
  27.8 32.2 %copy-start.9 = (bf16[128,2304]{1,0:T(8,128)(2,1)}, bf16[128,2304]{1,0:T(8,128)(2,1)S(1)}, u32[]{:S(2)}) copy-start(bf16[128,2304]{1,0:T(8,128)(2,1)S(1)} %collective-permute-done.2.refs_2_) | copy-start | bytes 1769476
  27.9 34.0 %copy-start.10 = (bf16[128,2304]{1,0:T(8,128)(2,1)}, bf16[128,2304]{1,0:T(8,128)(2,1)S(1)}, u32[]{:S(2)}) copy-start(bf16[128,2304]{1,0:T(8,128)(2,1)S(1)} %collective-permute-done.3.refs_3_) | copy-start | bytes 1769476
  27.9 15.1 %collective-permute-start.5 = (bf16[128,2304]{1,0:T(8,128)(2,1)S(1)}, bf16[128,2304]{1,0:T(8,128)(2,1)}, u32[]{:S(2)}, u32[]{:S(2)}) collective-permute-start(bf16[128,2304]{1,0:T(8,128)(2,1)S(1)} %collective-permute-done.3.refs_3_), channel_id=1, source_target_pairs={{0,6},{1,7},{2,0},{3,1},{4,2},{5,3},{6,4},{7,5},{8,14},{9,15},{10,... | collective-permute-start | bytes 1769480 | tf_op jit(solution)/shard_map/ppermute | solution.py:283
  31.2 17.6 %collective-permute-start.6 = (bf16[128,2304]{1,0:T(8,128)(2,1)S(1)}, bf16[128,2304]{1,0:T(8,128)(2,1)}, u32[]{:S(2)}, u32[]{:S(2)}) collective-permute-start(bf16[128,2304]{1,0:T(8,128)(2,1)S(1)} %collective-permute-done.2.refs_2_), channel_id=1, source_target_pairs={{0,2},{1,3},{2,4},{3,5},{4,6},{5,7},{6,0},{7,1},{8,10},{9,11},{10,... | collective-permute-start | bytes 1769480 | tf_op jit(solution)/shard_map/ppermute | solution.py:279
  31.2 2.1 %collective-permute-start.4 = (bf16[256,1024]{1,0:T(8,128)(2,1)}, bf16[256,1024]{1,0:T(8,128)(2,1)S(1)}, u32[]{:S(2)}, u32[]{:S(2)}) collective-permute-start(bf16[256,1024]{1,0:T(8,128)(2,1)} %get-tuple-element.54), channel_id=1, source_target_pairs={{0,1},{1,0},{2,3},{3,2},{4,5},{5,4},{6,7},{7,6},{8,9},{9,8},{10,11... | collective-permute-start | bytes 1572872 | tf_op jit(solution)/shard_map/ppermute | solution.py:291
  31.2 27.9 %collective-permute-start.8 = (bf16[128,2304]{1,0:T(8,128)(2,1)S(1)}, bf16[128,2304]{1,0:T(8,128)(2,1)}, u32[]{:S(2)}, u32[]{:S(2)}) collective-permute-start(bf16[128,2304]{1,0:T(8,128)(2,1)S(1)} %collective-permute-done.3.refs_3_), channel_id=1, source_target_pairs={{0,2},{1,3},{2,4},{3,5},{4,6},{5,7},{6,0},{7,1},{8,10},{9,11},{10,... | collective-permute-start | bytes 1769480 | tf_op jit(solution)/shard_map/ppermute | solution.py:279
  41.3 20.5 %copy-start.5 = (bf16[128,2304]{1,0:T(8,128)(2,1)S(1)}, bf16[128,2304]{1,0:T(8,128)(2,1)}, u32[]{:S(2)}) copy-start(bf16[128,2304]{1,0:T(8,128)(2,1)} %get-tuple-element.67) | copy-start | bytes 1769476
  48.8 12.2 %collective-permute-start.7 = (bf16[128,2304]{1,0:T(8,128)(2,1)}, bf16[128,2304]{1,0:T(8,128)(2,1)S(1)}, u32[]{:S(2)}, u32[]{:S(2)}) collective-permute-start(bf16[128,2304]{1,0:T(8,128)(2,1)} %collective-permute-done.5.refs_4_), channel_id=1, source_target_pairs={{0,6},{1,7},{2,0},{3,1},{4,2},{5,3},{6,4},{7,5},{8,14},{9,15},{10,... | collective-permute-start | bytes 1769480 | tf_op jit(solution)/shard_map/ppermute | solution.py:283
  48.8 13.1 %collective-permute-start.9 = (bf16[128,2304]{1,0:T(8,128)(2,1)}, bf16[128,2304]{1,0:T(8,128)(2,1)S(1)}, u32[]{:S(2)}, u32[]{:S(2)}) collective-permute-start(bf16[128,2304]{1,0:T(8,128)(2,1)} %get-tuple-element.68), channel_id=1, source_target_pairs={{0,8},{1,9},{2,10},{3,11},{4,12},{5,13},{6,14},{7,15},{8,0},{9,1},... | collective-permute-start | bytes 1769480 | tf_op jit(solution)/shard_map/ppermute | solution.py:287
  60.0 27.1 %collective-permute-start.11 = (bf16[128,2304]{1,0:T(8,128)(2,1)}, bf16[128,2304]{1,0:T(8,128)(2,1)S(1)}, u32[]{:S(2)}, u32[]{:S(2)}) collective-permute-start(bf16[128,2304]{1,0:T(8,128)(2,1)} %get-tuple-element.75), channel_id=1, source_target_pairs={{0,8},{1,9},{2,10},{3,11},{4,12},{5,13},{6,14},{7,15},{8,0},{9,1},... | collective-permute-start | bytes 1769480 | tf_op jit(solution)/shard_map/ppermute | solution.py:287
  62.0 25.1 %collective-permute-start.12 = (bf16[128,2304]{1,0:T(8,128)(2,1)S(1)}, bf16[128,2304]{1,0:T(8,128)(2,1)S(1)}, u32[]{:S(2)}, u32[]{:S(2)}) collective-permute-start(bf16[128,2304]{1,0:T(8,128)(2,1)S(1)} %add_convert_fusion.4), channel_id=1, source_target_pairs={{0,2},{1,3},{2,4},{3,5},{4,6},{5,7},{6,0},{7,1},{8,10},{9,11},{10,... | collective-permute-start | bytes 1769480 | tf_op jit(solution)/shard_map/ppermute | solution.py:279
  63.2 28.3 %all-to-all-start.1 = ((bf16[16,144,128]{2,1,0:T(8,128)(2,1)}), bf16[16,144,128]{2,1,0:T(8,128)(2,1)S(1)}, u32[]{:S(2)}, u32[]{:S(2)}) async-start(bf16[16,144,128]{2,1,0:T(8,128)(2,1)} %broadcast_in_dim.16), calls=%async_computation.1 | async-start | bytes 1179648 | tf_op jit(solution)/shard_map/all_to_all | solution.py:396
  72.8 14.6 %collective-permute-start.13 = (bf16[128,2304]{1,0:T(8,128)(2,1)}, bf16[128,2304]{1,0:T(8,128)(2,1)S(1)}, u32[]{:S(2)}, u32[]{:S(2)}) collective-permute-start(bf16[128,2304]{1,0:T(8,128)(2,1)} %get-tuple-element.78), channel_id=1, source_target_pairs={{0,6},{1,7},{2,0},{3,1},{4,2},{5,3},{6,4},{7,5},{8,14},{9,15},{10,... | collective-permute-start | bytes 1769480 | tf_op jit(solution)/shard_map/ppermute | solution.py:283
  86.5 9.6 %collective-permute-start.14 = (bf16[256,1024]{1,0:T(8,128)(2,1)}, bf16[256,1024]{1,0:T(8,128)(2,1)}, u32[]{:S(2)}, u32[]{:S(2)}) collective-permute-start(bf16[256,1024]{1,0:T(8,128)(2,1)} %get-tuple-element.81), channel_id=1, source_target_pairs={{0,1},{1,0},{2,3},{3,2},{4,5},{5,4},{6,7},{7,6},{8,9},{9,8},{10,11... | collective-permute-start | bytes 1572872 | tf_op jit(solution)/shard_map/ppermute | solution.py:291
  86.6 20.3 %collective-permute-start.10 = (bf16[256,2304]{1,0:T(8,128)(2,1)}, bf16[256,2304]{1,0:T(8,128)(2,1)S(1)}, u32[]{:S(2)}, u32[]{:S(2)}) collective-permute-start(bf16[256,2304]{1,0:T(8,128)(2,1)} %get-tuple-element.72), channel_id=1, source_target_pairs={{0,1},{1,0},{2,3},{3,2},{4,5},{5,4},{6,7},{7,6},{8,9},{9,8},{10,11... | collective-permute-start | bytes 3538952 | tf_op jit(solution)/shard_map/ppermute | solution.py:291
  88.3 19.8 %collective-permute-start.15 = (bf16[128,2304]{1,0:T(8,128)(2,1)}, bf16[128,2304]{1,0:T(8,128)(2,1)S(1)}, u32[]{:S(2)}, u32[]{:S(2)}) collective-permute-start(bf16[128,2304]{1,0:T(8,128)(2,1)} %get-tuple-element.88), channel_id=1, source_target_pairs={{0,6},{1,7},{2,0},{3,1},{4,2},{5,3},{6,4},{7,5},{8,14},{9,15},{10,... | collective-permute-start | bytes 1769480 | tf_op jit(solution)/shard_map/ppermute | solution.py:283
  88.8 19.4 %collective-permute-start.17 = (bf16[128,2304]{1,0:T(8,128)(2,1)S(1)}, bf16[128,2304]{1,0:T(8,128)(2,1)}, u32[]{:S(2)}, u32[]{:S(2)}) collective-permute-start(bf16[128,2304]{1,0:T(8,128)(2,1)S(1)} %add_convert_fusion.2), channel_id=1, source_target_pairs={{0,8},{1,9},{2,10},{3,11},{4,12},{5,13},{6,14},{7,15},{8,0},{9,1},... | collective-permute-start | bytes 1769480 | tf_op jit(solution)/shard_map/ppermute | solution.py:287
  89.8 18.4 %collective-permute-start.16 = (bf16[128,2304]{1,0:T(8,128)(2,1)S(1)}, bf16[128,2304]{1,0:T(8,128)(2,1)}, u32[]{:S(2)}, u32[]{:S(2)}) collective-permute-start(bf16[128,2304]{1,0:T(8,128)(2,1)S(1)} %add_convert_fusion.3), channel_id=1, source_target_pairs={{0,2},{1,3},{2,4},{3,5},{4,6},{5,7},{6,0},{7,1},{8,10},{9,11},{10,... | collective-permute-start | bytes 1769480 | tf_op jit(solution)/shard_map/ppermute | solution.py:279
  (10 other events, 54.2 us)
